TPU v7x, 512 devices: a whole 4x4x16 slice. The times are simulated.
512 devices in a mesh: tm: 32 (over z_lo, x, core), space: 16 (over z_hi, y).
Axes of the slice: x: 4, y: 4, z: 16 (z_hi: 4, z_lo: 4; z = z_hi * 4 + z_lo), core: 2. Of those that a mesh axis runs over, the one named last changes fastest.
Arguments:
- initial_state: float32 [768, 512], P('space'), may hold values from -6 to 6
- velocity: bfloat16 [768, 512], P('space'), may hold values from -0.5 to 0.5
- diffusion: bfloat16 [768, 512], P('space'), may hold values from 0.25 to 0.5
- forcing: bfloat16 [256, 768, 512], P('tm', 'space'), may hold values from -6 to 6
- implicit: float32 [512, 512], replicated, may hold values from 0 to 1
- coarse_implicit: float32 [512, 512], replicated, may hold values from 0 to 1
Outputs:
- solution: float32 [256, 768, 512], P('tm', 'space')
All inputs are finite; a program needn't handle non-finite values.
Results may differ from a plain program's by a relative error of at most 0.0003.
Values may be sent and summed in bfloat16 or wider, within the bound.
A program may use at most 64 MiB of HBM per device.

v0:
```python
import jax
import jax.numpy as jnp
from jax import lax
from jax.sharding import PartitionSpec as P

CYCLES = 2


HIGHEST = lax.Precision.HIGHEST


def with_halo(cells, sides, width):
    for axis, dim in sides:
        count = lax.axis_size(axis)
        head = lax.slice_in_dim(cells, 0, width, axis=dim)
        tail = lax.slice_in_dim(cells, cells.shape[dim] - width, cells.shape[dim], axis=dim)
        cells = jnp.concatenate(
            [
                lax.ppermute(tail, axis, [(i, (i + 1) % count) for i in range(count)]),
                cells,
                lax.ppermute(head, axis, [((i + 1) % count, i) for i in range(count)]),
            ],
            axis=dim,
        )
    return cells


def from_behind(block, axis, distance):
    devices = range(lax.axis_size(axis))
    route = [(i - distance, i) for i in devices if i - distance in devices]
    return lax.ppermute(block, axis, route)


def stencil_weights(velocity, diffusion):
    moving = velocity.astype(jnp.float32)
    spread = diffusion.astype(jnp.float32)
    return (spread + 0.5 * moving, 1.0 - 2.0 * spread, spread - 0.5 * moving)


def apply_matrix(field, matrix):
    return jnp.dot(field, matrix, precision=HIGHEST, preferred_element_type=jnp.float32)


def per_device(initial_state, velocity, diffusion, forcing, implicit, coarse_implicit):
    block_steps = forcing.shape[0]
    weights = stencil_weights(velocity, diffusion)
    first_block = lax.axis_index("tm") == 0

    def relax_block(begin_state, step_count):
        values = []
        current = begin_state
        for offset in range(step_count):
            padded = with_halo(current, (("space", 0),), 1)
            summed = (
                weights[1] * current
                + weights[2] * padded[2:]
                + weights[0] * padded[:-2]
                + forcing[offset].astype(jnp.float32)
            )
            current = apply_matrix(summed, implicit)
            values.append(current)
        return values

    def previous(end_values):
        arrived = from_behind(end_values, "tm", 1)
        return jnp.where(first_block, initial_state, arrived)

    end_values = jnp.zeros_like(initial_state)
    for repeat in range(CYCLES):
        if repeat == 0:
            begin_state = jnp.where(first_block, initial_state, jnp.zeros_like(initial_state))
        else:
            begin_state = previous(end_values)
        end_values = relax_block(begin_state, block_steps)[-1]
        residual = relax_block(previous(end_values), block_steps)[-1] - end_values
        gathered = lax.all_gather(
            residual[None].astype(jnp.bfloat16), "tm", axis=0, tiled=True
        ).astype(jnp.float32)

        def coarse_turn(source, carried):
            return apply_matrix(carried, coarse_implicit) + gathered[source]

        end_values = end_values + lax.fori_loop(
            1, lax.axis_index("tm") + 1, coarse_turn, gathered[0]
        )
    values = relax_block(previous(end_values), block_steps - 1)
    return jnp.stack(values + [end_values], axis=0)


def solution(mesh):
    in_specs = (
        P("space", None),
        P("space", None),
        P("space", None),
        P("tm", "space", None),
        P(),
        P(),
    )
    out_specs = P("tm", "space", None)
    return jax.shard_map(
        per_device, mesh=mesh, in_specs=in_specs, out_specs=out_specs, check_vma=False
    )
```

profile of v0, /device:TPU:102, one launch (start us, length us, event | category | flops | bytes accessed | tf_op | source)
XLA Modules:
  0.0 854.1 jit_solution(8484713304822959292)
XLA Ops:
  6.6 12.6 %collective-permute-start = (f32[1,512]{1,0:T(1,128)S(1)}, f32[1,512]{1,0:T(1,128)S(1)}, u32[]{:S(2)}, u32[]{:S(2)}) collective-permute-start(f32[1,512]{1,0:T(1,128)S(1)} %get-tuple-element.159), channel_id=1, source_target_pairs={{1,0},{2,1},{3,2},{4,3},{5,4},{6,5},{7,6},{8,7},{9,8},{10,9},{11,1... | collective-permute-start | bytes 6152 | tf_op jit(solution)/shard_map/ppermute | solution.py:21
  21.2 9.6 %collective-permute-done.1 = f32[1,512]{1,0:T(1,128)S(1)} collective-permute-done((f32[1,512]{1,0:T(1,128)S(1)}, f32[1,512]{1,0:T(1,128)S(1)}, u32[]{:S(2)}, u32[]{:S(2)}) %collective-permute-start.1) | collective-permute-done | bytes 2080 | tf_op jit(solution)/shard_map/ppermute | solution.py:19
  34.3 3.9 collective-permute-start.3
  38.2 7.6 collective-permute-done.3
  49.4 3.9 collective-permute-start.5
  53.3 7.6 collective-permute-done.5
  64.4 3.9 collective-permute-start.7
  68.4 7.6 collective-permute-done.7
  83.6 7.6 collective-permute-done.9
  98.6 7.6 collective-permute-done.11
  113.6 7.6 collective-permute-done.13
  128.7 7.6 collective-permute-done.15
  139.7 4.0 collective-permute-done.16
  145.7 3.9 collective-permute-start.18
  149.6 7.6 collective-permute-done.18
  163.9 7.6 collective-permute-done.20
  174.2 3.9 collective-permute-start.22
  178.1 7.6 collective-permute-done.22
  192.3 7.6 collective-permute-done.24
  206.6 7.6 collective-permute-done.26
  216.9 3.9 collective-permute-start.28
  220.8 7.6 collective-permute-done.28
  231.1 4.1 collective-permute-start.30
  235.2 7.4 collective-permute-done.30
  245.3 4.1 collective-permute-start.32
  249.4 7.6 collective-permute-done.32
  258.4 55.3 %all-gather.5.cloned.1.call-done = bf16[1536,512]{1,0:T(8,128)(2,1)} async-done(((bf16[48,512]{1,0:T(8,128)(2,1)}), bf16[1536,512]{1,0:T(8,128)(2,1)}) %all-gather.5.cloned.1.call-update) | async-done | bytes 1572880 | tf_op jit(solution)/shard_map/all_gather | solution.py:76
  318.1 50.1 %while.20 = (s32[]{:T(128)}, f32[48,512]{1,0:T(8,128)S(1)}, s32[]{:T(128)}, f32[512,512]{1,0:T(8,128)S(1)}, f32[32,48,512]{2,1,0:T(8,128)}, /*index=5*/s32[]{:T(128)}, s32[]{:T(128)}, s32[]{:T(128)}) while((s32[]{:T(128)}, f32[48,512]{1,0:T(8,128)S(1)}, s32[]{:T(128)}, f32[512,512]{1,0:T(8,128)S(1)}, f32[32,48,512]{2,1,0:T(8,128)}, ...), condition=%wide.region_1.2_spmd, body=%wide.region_0.1_spmd.sunk | while | flops 151019520 | bytes 1540219 | solution.py:83
  374.2 9.1 %collective-permute-start.34 = (f32[1,512]{1,0:T(1,128)S(1)}, f32[1,512]{1,0:T(1,128)S(1)}, u32[]{:S(2)}, u32[]{:S(2)}) collective-permute-start(f32[1,512]{1,0:T(1,128)S(1)} %get-tuple-element.127), channel_id=1, source_target_pairs={{1,0},{2,1},{3,2},{4,3},{5,4},{6,5},{7,6},{8,7},{9,8},{10,9},{11,1... | collective-permute-start | bytes 6152 | tf_op jit(solution)/shard_map/ppermute | solution.py:21
  385.2 9.6 %collective-permute-done.35 = f32[1,512]{1,0:T(1,128)S(1)} collective-permute-done((f32[1,512]{1,0:T(1,128)S(1)}, f32[1,512]{1,0:T(1,128)S(1)}, u32[]{:S(2)}, u32[]{:S(2)}) %collective-permute-start.35) | collective-permute-done | bytes 2080 | tf_op jit(solution)/shard_map/ppermute | solution.py:19
  402.3 7.6 collective-permute-done.37
  417.3 7.6 collective-permute-done.39
  428.4 3.9 collective-permute-start.41
  432.3 7.6 collective-permute-done.41
  447.4 7.6 collective-permute-done.43
  458.4 3.9 collective-permute-start.45
  462.4 7.6 collective-permute-done.45
  477.4 7.6 collective-permute-done.47
  492.4 7.6 collective-permute-done.49
  503.5 4.0 collective-permute-done.50
  513.4 7.6 collective-permute-done.52
  523.7 3.9 collective-permute-start.54
  527.6 7.6 collective-permute-done.54
  541.9 7.6 collective-permute-done.56
  556.1 7.6 collective-permute-done.58
  566.4 4.1 collective-permute-start.60
  570.6 7.3 collective-permute-done.60
  584.6 7.6 collective-permute-done.62
  594.9 3.9 collective-permute-start.64
  598.8 7.6 collective-permute-done.64
  613.0 7.6 collective-permute-done.66
  622.0 56.5 %all-gather.7.cloned.1.call-done = bf16[1536,512]{1,0:T(8,128)(2,1)} async-done(((bf16[48,512]{1,0:T(8,128)(2,1)}), bf16[1536,512]{1,0:T(8,128)(2,1)}) %all-gather.7.cloned.1.call-update) | async-done | bytes 1572880 | tf_op jit(solution)/shard_map/all_gather | solution.py:76
  682.8 50.1 %while.21 = (s32[]{:T(128)}, f32[48,512]{1,0:T(8,128)S(1)}, s32[]{:T(128)}, f32[512,512]{1,0:T(8,128)S(1)}, f32[32,48,512]{2,1,0:T(8,128)}, /*index=5*/s32[]{:T(128)}, s32[]{:T(128)}, s32[]{:T(128)}) while((s32[]{:T(128)}, f32[48,512]{1,0:T(8,128)S(1)}, s32[]{:T(128)}, f32[512,512]{1,0:T(8,128)S(1)}, f32[32,48,512]{2,1,0:T(8,128)}, ...), condition=%wide.region_3.4_spmd, body=%wide.region_2.3_spmd.sunk | while | flops 151019520 | bytes 1540219 | solution.py:83
  738.9 9.1 %collective-permute-start.68 = (f32[1,512]{1,0:T(1,128)S(1)}, f32[1,512]{1,0:T(1,128)S(1)}, u32[]{:S(2)}, u32[]{:S(2)}) collective-permute-start(f32[1,512]{1,0:T(1,128)S(1)} %get-tuple-element.95), channel_id=1, source_target_pairs={{1,0},{2,1},{3,2},{4,3},{5,4},{6,5},{7,6},{8,7},{9,8},{10,9},{11,1... | collective-permute-start | bytes 6152 | tf_op jit(solution)/shard_map/ppermute | solution.py:21
  750.0 9.6 %collective-permute-done.69 = f32[1,512]{1,0:T(1,128)S(1)} collective-permute-done((f32[1,512]{1,0:T(1,128)S(1)}, f32[1,512]{1,0:T(1,128)S(1)}, u32[]{:S(2)}, u32[]{:S(2)}) %collective-permute-start.69) | collective-permute-done | bytes 2080 | tf_op jit(solution)/shard_map/ppermute | solution.py:19
  762.2 3.9 collective-permute-start.71
  766.2 7.6 collective-permute-done.71
  780.4 7.6 collective-permute-done.73
  794.7 7.6 collective-permute-done.75
  804.9 3.9 collective-permute-start.77
  808.9 7.6 collective-permute-done.77
  819.2 3.9 collective-permute-start.79
  823.1 7.6 collective-permute-done.79
  837.3 7.6 collective-permute-done.81
  (332 shorter events, 322.4 us)
Async XLA Ops:
  6.5 307.2 %all-gather.5.cloned.1.call-start = ((), (), s32[]{:S(2)}) async-start(), calls=%async_computation | async-start | bytes 1622016 | tf_op jit(solution)/shard_map/all_gather | solution.py:76
  6.6 14.6 %collective-permute-start = (f32[1,512]{1,0:T(1,128)S(1)}, f32[1,512]{1,0:T(1,128)S(1)}, u32[]{:S(2)}, u32[]{:S(2)}) collective-permute-start(f32[1,512]{1,0:T(1,128)S(1)} %get-tuple-element.159), channel_id=1, source_target_pairs={{1,0},{2,1},{3,2},{4,3},{5,4},{6,5},{7,6},{8,7},{9,8},{10,9},{11,1... | collective-permute-start | bytes 6152 | tf_op jit(solution)/shard_map/ppermute | solution.py:21
  19.2 11.5 %collective-permute-start.1 = (f32[1,512]{1,0:T(1,128)S(1)}, f32[1,512]{1,0:T(1,128)S(1)}, u32[]{:S(2)}, u32[]{:S(2)}) collective-permute-start(f32[1,512]{1,0:T(1,128)S(1)} %get-tuple-element.160), channel_id=1, source_target_pairs={{0,1},{1,2},{2,3},{3,4},{4,5},{5,6},{6,7},{7,8},{8,9},{9,10},{10,1... | collective-permute-start | bytes 6152 | tf_op jit(solution)/shard_map/ppermute | solution.py:19
  32.4 5.9 collective-permute-start.2
  34.3 11.5 %collective-permute-start.3 = (f32[1,512]{1,0:T(1,128)S(1)}, f32[1,512]{1,0:T(1,128)S(1)}, u32[]{:S(2)}, u32[]{:S(2)}) collective-permute-start(f32[1,512]{1,0:T(1,128)S(1)} %get-tuple-element.158), channel_id=1, source_target_pairs={{0,1},{1,2},{2,3},{3,4},{4,5},{5,6},{6,7},{7,8},{8,9},{9,10},{10,1... | collective-permute-start | bytes 6152 | tf_op jit(solution)/shard_map/ppermute | solution.py:19
  47.4 5.9 collective-permute-start.4
  49.4 11.5 %collective-permute-start.5 = (f32[1,512]{1,0:T(1,128)S(1)}, f32[1,512]{1,0:T(1,128)S(1)}, u32[]{:S(2)}, u32[]{:S(2)}) collective-permute-start(f32[1,512]{1,0:T(1,128)S(1)} %get-tuple-element.156), channel_id=1, source_target_pairs={{0,1},{1,2},{2,3},{3,4},{4,5},{5,6},{6,7},{7,8},{8,9},{9,10},{10,1... | collective-permute-start | bytes 6152 | tf_op jit(solution)/shard_map/ppermute | solution.py:19
  64.4 11.5 %collective-permute-start.7 = (f32[1,512]{1,0:T(1,128)S(1)}, f32[1,512]{1,0:T(1,128)S(1)}, u32[]{:S(2)}, u32[]{:S(2)}) collective-permute-start(f32[1,512]{1,0:T(1,128)S(1)} %get-tuple-element.154), channel_id=1, source_target_pairs={{0,1},{1,2},{2,3},{3,4},{4,5},{5,6},{6,7},{7,8},{8,9},{9,10},{10,1... | collective-permute-start | bytes 6152 | tf_op jit(solution)/shard_map/ppermute | solution.py:19
  77.6 6.0 collective-permute-start.8
  79.6 11.5 %collective-permute-start.9 = (f32[1,512]{1,0:T(1,128)S(1)}, f32[1,512]{1,0:T(1,128)S(1)}, u32[]{:S(2)}, u32[]{:S(2)}) collective-permute-start(f32[1,512]{1,0:T(1,128)S(1)} %get-tuple-element.152), channel_id=1, source_target_pairs={{0,1},{1,2},{2,3},{3,4},{4,5},{5,6},{6,7},{7,8},{8,9},{9,10},{10,1... | collective-permute-start | bytes 6152 | tf_op jit(solution)/shard_map/ppermute | solution.py:19
  92.7 5.9 collective-permute-start.10
  94.7 11.5 %collective-permute-start.11 = (f32[1,512]{1,0:T(1,128)S(1)}, f32[1,512]{1,0:T(1,128)S(1)}, u32[]{:S(2)}, u32[]{:S(2)}) collective-permute-start(f32[1,512]{1,0:T(1,128)S(1)} %get-tuple-element.150), channel_id=1, source_target_pairs={{0,1},{1,2},{2,3},{3,4},{4,5},{5,6},{6,7},{7,8},{8,9},{9,10},{10,1... | collective-permute-start | bytes 6152 | tf_op jit(solution)/shard_map/ppermute | solution.py:19
  109.7 11.5 %collective-permute-start.13 = (f32[1,512]{1,0:T(1,128)S(1)}, f32[1,512]{1,0:T(1,128)S(1)}, u32[]{:S(2)}, u32[]{:S(2)}) collective-permute-start(f32[1,512]{1,0:T(1,128)S(1)} %get-tuple-element.148), channel_id=1, source_target_pairs={{0,1},{1,2},{2,3},{3,4},{4,5},{5,6},{6,7},{7,8},{8,9},{9,10},{10,1... | collective-permute-start | bytes 6152 | tf_op jit(solution)/shard_map/ppermute | solution.py:19
  122.8 5.9 collective-permute-start.14
  124.7 11.5 %collective-permute-start.15 = (f32[1,512]{1,0:T(1,128)S(1)}, f32[1,512]{1,0:T(1,128)S(1)}, u32[]{:S(2)}, u32[]{:S(2)}) collective-permute-start(f32[1,512]{1,0:T(1,128)S(1)} %get-tuple-element.146), channel_id=1, source_target_pairs={{0,1},{1,2},{2,3},{3,4},{4,5},{5,6},{6,7},{7,8},{8,9},{9,10},{10,1... | collective-permute-start | bytes 6152 | tf_op jit(solution)/shard_map/ppermute | solution.py:19
  137.8 5.9 collective-permute-start.16
  143.8 5.9 collective-permute-start.17
  145.7 11.5 %collective-permute-start.18 = (f32[1,512]{1,0:T(1,128)S(1)}, f32[1,512]{1,0:T(1,128)S(1)}, u32[]{:S(2)}, u32[]{:S(2)}) collective-permute-start(f32[1,512]{1,0:T(1,128)S(1)} %get-tuple-element.144), channel_id=1, source_target_pairs={{0,1},{1,2},{2,3},{3,4},{4,5},{5,6},{6,7},{7,8},{8,9},{9,10},{10,1... | collective-permute-start | bytes 6152 | tf_op jit(solution)/shard_map/ppermute | solution.py:19
  159.9 11.5 %collective-permute-start.20 = (f32[1,512]{1,0:T(1,128)S(1)}, f32[1,512]{1,0:T(1,128)S(1)}, u32[]{:S(2)}, u32[]{:S(2)}) collective-permute-start(f32[1,512]{1,0:T(1,128)S(1)} %get-tuple-element.142), channel_id=1, source_target_pairs={{0,1},{1,2},{2,3},{3,4},{4,5},{5,6},{6,7},{7,8},{8,9},{9,10},{10,1... | collective-permute-start | bytes 6152 | tf_op jit(solution)/shard_map/ppermute | solution.py:19
  172.2 5.9 collective-permute-start.21
  174.2 11.5 %collective-permute-start.22 = (f32[1,512]{1,0:T(1,128)S(1)}, f32[1,512]{1,0:T(1,128)S(1)}, u32[]{:S(2)}, u32[]{:S(2)}) collective-permute-start(f32[1,512]{1,0:T(1,128)S(1)} %get-tuple-element.140), channel_id=1, source_target_pairs={{0,1},{1,2},{2,3},{3,4},{4,5},{5,6},{6,7},{7,8},{8,9},{9,10},{10,1... | collective-permute-start | bytes 6152 | tf_op jit(solution)/shard_map/ppermute | solution.py:19
  186.5 5.9 collective-permute-start.23
  188.4 11.5 %collective-permute-start.24 = (f32[1,512]{1,0:T(1,128)S(1)}, f32[1,512]{1,0:T(1,128)S(1)}, u32[]{:S(2)}, u32[]{:S(2)}) collective-permute-start(f32[1,512]{1,0:T(1,128)S(1)} %get-tuple-element.138), channel_id=1, source_target_pairs={{0,1},{1,2},{2,3},{3,4},{4,5},{5,6},{6,7},{7,8},{8,9},{9,10},{10,1... | collective-permute-start | bytes 6152 | tf_op jit(solution)/shard_map/ppermute | solution.py:19
  200.7 5.9 collective-permute-start.25
  202.6 11.5 %collective-permute-start.26 = (f32[1,512]{1,0:T(1,128)S(1)}, f32[1,512]{1,0:T(1,128)S(1)}, u32[]{:S(2)}, u32[]{:S(2)}) collective-permute-start(f32[1,512]{1,0:T(1,128)S(1)} %get-tuple-element.136), channel_id=1, source_target_pairs={{0,1},{1,2},{2,3},{3,4},{4,5},{5,6},{6,7},{7,8},{8,9},{9,10},{10,1... | collective-permute-start | bytes 6152 | tf_op jit(solution)/shard_map/ppermute | solution.py:19
  214.9 5.9 collective-permute-start.27
  216.9 11.5 %collective-permute-start.28 = (f32[1,512]{1,0:T(1,128)S(1)}, f32[1,512]{1,0:T(1,128)S(1)}, u32[]{:S(2)}, u32[]{:S(2)}) collective-permute-start(f32[1,512]{1,0:T(1,128)S(1)} %get-tuple-element.134), channel_id=1, source_target_pairs={{0,1},{1,2},{2,3},{3,4},{4,5},{5,6},{6,7},{7,8},{8,9},{9,10},{10,1... | collective-permute-start | bytes 6152 | tf_op jit(solution)/shard_map/ppermute | solution.py:19
  229.2 6.0 collective-permute-start.29
  231.1 11.5 %collective-permute-start.30 = (f32[1,512]{1,0:T(1,128)S(1)}, f32[1,512]{1,0:T(1,128)S(1)}, u32[]{:S(2)}, u32[]{:S(2)}) collective-permute-start(f32[1,512]{1,0:T(1,128)S(1)} %get-tuple-element.132), channel_id=1, source_target_pairs={{0,1},{1,2},{2,3},{3,4},{4,5},{5,6},{6,7},{7,8},{8,9},{9,10},{10,1... | collective-permute-start | bytes 6152 | tf_op jit(solution)/shard_map/ppermute | solution.py:19
  243.4 6.0 collective-permute-start.31
  245.3 11.6 %collective-permute-start.32 = (f32[1,512]{1,0:T(1,128)S(1)}, f32[1,512]{1,0:T(1,128)S(1)}, u32[]{:S(2)}, u32[]{:S(2)}) collective-permute-start(f32[1,512]{1,0:T(1,128)S(1)} %get-tuple-element.130), channel_id=1, source_target_pairs={{0,1},{1,2},{2,3},{3,4},{4,5},{5,6},{6,7},{7,8},{8,9},{9,10},{10,1... | collective-permute-start | bytes 6152 | tf_op jit(solution)/shard_map/ppermute | solution.py:19
  258.4 420.1 %all-gather.7.cloned.1.call-start = ((), (), s32[]{:S(2)}) async-start(), calls=%async_computation.1 | async-start | bytes 1622016 | tf_op jit(solution)/shard_map/all_gather | solution.py:76
  368.2 5.9 collective-permute-start.33
  374.2 11.0 %collective-permute-start.34 = (f32[1,512]{1,0:T(1,128)S(1)}, f32[1,512]{1,0:T(1,128)S(1)}, u32[]{:S(2)}, u32[]{:S(2)}) collective-permute-start(f32[1,512]{1,0:T(1,128)S(1)} %get-tuple-element.127), channel_id=1, source_target_pairs={{1,0},{2,1},{3,2},{4,3},{5,4},{6,5},{7,6},{8,7},{9,8},{10,9},{11,1... | collective-permute-start | bytes 6152 | tf_op jit(solution)/shard_map/ppermute | solution.py:21
  383.3 11.5 %collective-permute-start.35 = (f32[1,512]{1,0:T(1,128)S(1)}, f32[1,512]{1,0:T(1,128)S(1)}, u32[]{:S(2)}, u32[]{:S(2)}) collective-permute-start(f32[1,512]{1,0:T(1,128)S(1)} %get-tuple-element.128), channel_id=1, source_target_pairs={{0,1},{1,2},{2,3},{3,4},{4,5},{5,6},{6,7},{7,8},{8,9},{9,10},{10,1... | collective-permute-start | bytes 6152 | tf_op jit(solution)/shard_map/ppermute | solution.py:19
  396.4 5.9 collective-permute-start.36
  398.3 11.5 %collective-permute-start.37 = (f32[1,512]{1,0:T(1,128)S(1)}, f32[1,512]{1,0:T(1,128)S(1)}, u32[]{:S(2)}, u32[]{:S(2)}) collective-permute-start(f32[1,512]{1,0:T(1,128)S(1)} %get-tuple-element.126), channel_id=1, source_target_pairs={{0,1},{1,2},{2,3},{3,4},{4,5},{5,6},{6,7},{7,8},{8,9},{9,10},{10,1... | collective-permute-start | bytes 6152 | tf_op jit(solution)/shard_map/ppermute | solution.py:19
  411.4 5.9 collective-permute-start.38
  413.4 11.5 %collective-permute-start.39 = (f32[1,512]{1,0:T(1,128)S(1)}, f32[1,512]{1,0:T(1,128)S(1)}, u32[]{:S(2)}, u32[]{:S(2)}) collective-permute-start(f32[1,512]{1,0:T(1,128)S(1)} %get-tuple-element.124), channel_id=1, source_target_pairs={{0,1},{1,2},{2,3},{3,4},{4,5},{5,6},{6,7},{7,8},{8,9},{9,10},{10,1... | collective-permute-start | bytes 6152 | tf_op jit(solution)/shard_map/ppermute | solution.py:19
  426.5 5.9 collective-permute-start.40
  428.4 11.5 %collective-permute-start.41 = (f32[1,512]{1,0:T(1,128)S(1)}, f32[1,512]{1,0:T(1,128)S(1)}, u32[]{:S(2)}, u32[]{:S(2)}) collective-permute-start(f32[1,512]{1,0:T(1,128)S(1)} %get-tuple-element.122), channel_id=1, source_target_pairs={{0,1},{1,2},{2,3},{3,4},{4,5},{5,6},{6,7},{7,8},{8,9},{9,10},{10,1... | collective-permute-start | bytes 6152 | tf_op jit(solution)/shard_map/ppermute | solution.py:19
  443.4 11.5 %collective-permute-start.43 = (f32[1,512]{1,0:T(1,128)S(1)}, f32[1,512]{1,0:T(1,128)S(1)}, u32[]{:S(2)}, u32[]{:S(2)}) collective-permute-start(f32[1,512]{1,0:T(1,128)S(1)} %get-tuple-element.120), channel_id=1, source_target_pairs={{0,1},{1,2},{2,3},{3,4},{4,5},{5,6},{6,7},{7,8},{8,9},{9,10},{10,1... | collective-permute-start | bytes 6152 | tf_op jit(solution)/shard_map/ppermute | solution.py:19
  458.4 11.5 %collective-permute-start.45 = (f32[1,512]{1,0:T(1,128)S(1)}, f32[1,512]{1,0:T(1,128)S(1)}, u32[]{:S(2)}, u32[]{:S(2)}) collective-permute-start(f32[1,512]{1,0:T(1,128)S(1)} %get-tuple-element.118), channel_id=1, source_target_pairs={{0,1},{1,2},{2,3},{3,4},{4,5},{5,6},{6,7},{7,8},{8,9},{9,10},{10,1... | collective-permute-start | bytes 6152 | tf_op jit(solution)/shard_map/ppermute | solution.py:19
  473.5 11.5 %collective-permute-start.47 = (f32[1,512]{1,0:T(1,128)S(1)}, f32[1,512]{1,0:T(1,128)S(1)}, u32[]{:S(2)}, u32[]{:S(2)}) collective-permute-start(f32[1,512]{1,0:T(1,128)S(1)} %get-tuple-element.116), channel_id=1, source_target_pairs={{0,1},{1,2},{2,3},{3,4},{4,5},{5,6},{6,7},{7,8},{8,9},{9,10},{10,1... | collective-permute-start | bytes 6152 | tf_op jit(solution)/shard_map/ppermute | solution.py:19
  488.5 11.5 %collective-permute-start.49 = (f32[1,512]{1,0:T(1,128)S(1)}, f32[1,512]{1,0:T(1,128)S(1)}, u32[]{:S(2)}, u32[]{:S(2)}) collective-permute-start(f32[1,512]{1,0:T(1,128)S(1)} %get-tuple-element.114), channel_id=1, source_target_pairs={{0,1},{1,2},{2,3},{3,4},{4,5},{5,6},{6,7},{7,8},{8,9},{9,10},{10,1... | collective-permute-start | bytes 6152 | tf_op jit(solution)/shard_map/ppermute | solution.py:19
  501.6 5.9 collective-permute-start.50
  509.5 11.5 %collective-permute-start.52 = (f32[1,512]{1,0:T(1,128)S(1)}, f32[1,512]{1,0:T(1,128)S(1)}, u32[]{:S(2)}, u32[]{:S(2)}) collective-permute-start(f32[1,512]{1,0:T(1,128)S(1)} %get-tuple-element.112), channel_id=1, source_target_pairs={{0,1},{1,2},{2,3},{3,4},{4,5},{5,6},{6,7},{7,8},{8,9},{9,10},{10,1... | collective-permute-start | bytes 6152 | tf_op jit(solution)/shard_map/ppermute | solution.py:19
  523.7 11.5 %collective-permute-start.54 = (f32[1,512]{1,0:T(1,128)S(1)}, f32[1,512]{1,0:T(1,128)S(1)}, u32[]{:S(2)}, u32[]{:S(2)}) collective-permute-start(f32[1,512]{1,0:T(1,128)S(1)} %get-tuple-element.110), channel_id=1, source_target_pairs={{0,1},{1,2},{2,3},{3,4},{4,5},{5,6},{6,7},{7,8},{8,9},{9,10},{10,1... | collective-permute-start | bytes 6152 | tf_op jit(solution)/shard_map/ppermute | solution.py:19
  537.9 11.5 %collective-permute-start.56 = (f32[1,512]{1,0:T(1,128)S(1)}, f32[1,512]{1,0:T(1,128)S(1)}, u32[]{:S(2)}, u32[]{:S(2)}) collective-permute-start(f32[1,512]{1,0:T(1,128)S(1)} %get-tuple-element.108), channel_id=1, source_target_pairs={{0,1},{1,2},{2,3},{3,4},{4,5},{5,6},{6,7},{7,8},{8,9},{9,10},{10,1... | collective-permute-start | bytes 6152 | tf_op jit(solution)/shard_map/ppermute | solution.py:19
  552.2 11.5 %collective-permute-start.58 = (f32[1,512]{1,0:T(1,128)S(1)}, f32[1,512]{1,0:T(1,128)S(1)}, u32[]{:S(2)}, u32[]{:S(2)}) collective-permute-start(f32[1,512]{1,0:T(1,128)S(1)} %get-tuple-element.106), channel_id=1, source_target_pairs={{0,1},{1,2},{2,3},{3,4},{4,5},{5,6},{6,7},{7,8},{8,9},{9,10},{10,1... | collective-permute-start | bytes 6152 | tf_op jit(solution)/shard_map/ppermute | solution.py:19
  564.5 6.1 collective-permute-start.59
  566.4 11.5 %collective-permute-start.60 = (f32[1,512]{1,0:T(1,128)S(1)}, f32[1,512]{1,0:T(1,128)S(1)}, u32[]{:S(2)}, u32[]{:S(2)}) collective-permute-start(f32[1,512]{1,0:T(1,128)S(1)} %get-tuple-element.104), channel_id=1, source_target_pairs={{0,1},{1,2},{2,3},{3,4},{4,5},{5,6},{6,7},{7,8},{8,9},{9,10},{10,1... | collective-permute-start | bytes 6152 | tf_op jit(solution)/shard_map/ppermute | solution.py:19
  580.6 11.5 %collective-permute-start.62 = (f32[1,512]{1,0:T(1,128)S(1)}, f32[1,512]{1,0:T(1,128)S(1)}, u32[]{:S(2)}, u32[]{:S(2)}) collective-permute-start(f32[1,512]{1,0:T(1,128)S(1)} %get-tuple-element.102), channel_id=1, source_target_pairs={{0,1},{1,2},{2,3},{3,4},{4,5},{5,6},{6,7},{7,8},{8,9},{9,10},{10,1... | collective-permute-start | bytes 6152 | tf_op jit(solution)/shard_map/ppermute | solution.py:19
  594.9 11.5 %collective-permute-start.64 = (f32[1,512]{1,0:T(1,128)S(1)}, f32[1,512]{1,0:T(1,128)S(1)}, u32[]{:S(2)}, u32[]{:S(2)}) collective-permute-start(f32[1,512]{1,0:T(1,128)S(1)} %get-tuple-element.100), channel_id=1, source_target_pairs={{0,1},{1,2},{2,3},{3,4},{4,5},{5,6},{6,7},{7,8},{8,9},{9,10},{10,1... | collective-permute-start | bytes 6152 | tf_op jit(solution)/shard_map/ppermute | solution.py:19
  609.1 11.5 %collective-permute-start.66 = (f32[1,512]{1,0:T(1,128)S(1)}, f32[1,512]{1,0:T(1,128)S(1)}, u32[]{:S(2)}, u32[]{:S(2)}) collective-permute-start(f32[1,512]{1,0:T(1,128)S(1)} %get-tuple-element.98), channel_id=1, source_target_pairs={{0,1},{1,2},{2,3},{3,4},{4,5},{5,6},{6,7},{7,8},{8,9},{9,10},{10,1... | collective-permute-start | bytes 6152 | tf_op jit(solution)/shard_map/ppermute | solution.py:19
  732.9 5.9 collective-permute-start.67
  738.9 11.0 %collective-permute-start.68 = (f32[1,512]{1,0:T(1,128)S(1)}, f32[1,512]{1,0:T(1,128)S(1)}, u32[]{:S(2)}, u32[]{:S(2)}) collective-permute-start(f32[1,512]{1,0:T(1,128)S(1)} %get-tuple-element.95), channel_id=1, source_target_pairs={{1,0},{2,1},{3,2},{4,3},{5,4},{6,5},{7,6},{8,7},{9,8},{10,9},{11,1... | collective-permute-start | bytes 6152 | tf_op jit(solution)/shard_map/ppermute | solution.py:21
  748.0 11.5 %collective-permute-start.69 = (f32[1,512]{1,0:T(1,128)S(1)}, f32[1,512]{1,0:T(1,128)S(1)}, u32[]{:S(2)}, u32[]{:S(2)}) collective-permute-start(f32[1,512]{1,0:T(1,128)S(1)} %get-tuple-element.96), channel_id=1, source_target_pairs={{0,1},{1,2},{2,3},{3,4},{4,5},{5,6},{6,7},{7,8},{8,9},{9,10},{10,1... | collective-permute-start | bytes 6152 | tf_op jit(solution)/shard_map/ppermute | solution.py:19
  762.2 11.5 %collective-permute-start.71 = (f32[1,512]{1,0:T(1,128)S(1)}, f32[1,512]{1,0:T(1,128)S(1)}, u32[]{:S(2)}, u32[]{:S(2)}) collective-permute-start(f32[1,512]{1,0:T(1,128)S(1)} %get-tuple-element.94), channel_id=1, source_target_pairs={{0,1},{1,2},{2,3},{3,4},{4,5},{5,6},{6,7},{7,8},{8,9},{9,10},{10,1... | collective-permute-start | bytes 6152 | tf_op jit(solution)/shard_map/ppermute | solution.py:19
  776.5 11.5 %collective-permute-start.73 = (f32[1,512]{1,0:T(1,128)S(1)}, f32[1,512]{1,0:T(1,128)S(1)}, u32[]{:S(2)}, u32[]{:S(2)}) collective-permute-start(f32[1,512]{1,0:T(1,128)S(1)} %get-tuple-element.92), channel_id=1, source_target_pairs={{0,1},{1,2},{2,3},{3,4},{4,5},{5,6},{6,7},{7,8},{8,9},{9,10},{10,1... | collective-permute-start | bytes 6152 | tf_op jit(solution)/shard_map/ppermute | solution.py:19
  790.7 11.5 %collective-permute-start.75 = (f32[1,512]{1,0:T(1,128)S(1)}, f32[1,512]{1,0:T(1,128)S(1)}, u32[]{:S(2)}, u32[]{:S(2)}) collective-permute-start(f32[1,512]{1,0:T(1,128)S(1)} %get-tuple-element.90), channel_id=1, source_target_pairs={{0,1},{1,2},{2,3},{3,4},{4,5},{5,6},{6,7},{7,8},{8,9},{9,10},{10,1... | collective-permute-start | bytes 6152 | tf_op jit(solution)/shard_map/ppermute | solution.py:19
  804.9 11.5 %collective-permute-start.77 = (f32[1,512]{1,0:T(1,128)S(1)}, f32[1,512]{1,0:T(1,128)S(1)}, u32[]{:S(2)}, u32[]{:S(2)}) collective-permute-start(f32[1,512]{1,0:T(1,128)S(1)} %get-tuple-element.88), channel_id=1, source_target_pairs={{0,1},{1,2},{2,3},{3,4},{4,5},{5,6},{6,7},{7,8},{8,9},{9,10},{10,1... | collective-permute-start | bytes 6152 | tf_op jit(solution)/shard_map/ppermute | solution.py:19
  819.2 11.5 %collective-permute-start.79 = (f32[1,512]{1,0:T(1,128)S(1)}, f32[1,512]{1,0:T(1,128)S(1)}, u32[]{:S(2)}, u32[]{:S(2)}) collective-permute-start(f32[1,512]{1,0:T(1,128)S(1)} %get-tuple-element.86), channel_id=1, source_target_pairs={{0,1},{1,2},{2,3},{3,4},{4,5},{5,6},{6,7},{7,8},{8,9},{9,10},{10,1... | collective-permute-start | bytes 6152 | tf_op jit(solution)/shard_map/ppermute | solution.py:19
  833.4 11.5 %collective-permute-start.81 = (f32[1,512]{1,0:T(1,128)S(1)}, f32[1,512]{1,0:T(1,128)S(1)}, u32[]{:S(2)}, u32[]{:S(2)}) collective-permute-start(f32[1,512]{1,0:T(1,128)S(1)} %get-tuple-element.84), channel_id=1, source_target_pairs={{0,1},{1,2},{2,3},{3,4},{4,5},{5,6},{6,7},{7,8},{8,9},{9,10},{10,1... | collective-permute-start | bytes 6152 | tf_op jit(solution)/shard_map/ppermute | solution.py:19
  (27 other events, 499.7 us)
Sparse Core Ops, SparseCore 0:
  258.5 55.1 all-gather.4
  622.1 56.3 all-gather.6
where the time goes:
time: 859 us; the launch traced here: 854 us
  waiting for transfers between devices  424 us (49%)
  starting transfers between devices  259 us (30%)
  matrix products  142 us (17%)
  between operations  15.1 us (2%)
    ppermute x39, waiting for transfers between devices, with_halo(): lax.ppermute(tail, axis, [(i, (i + 1) % count) for i in range(count)])  300 us
    ppermute x39, starting transfers between devices, with_halo(): lax.ppermute(tail, axis, [(i, (i + 1) % count) for i in range(count)])  147 us
    dot_general x99, matrix products, apply_matrix(): jnp.dot(field, matrix, precision=HIGHEST, preferred_element_type=jnp.floa...  142 us
    all_gather x2, waiting for transfers between devices, per_device(): lax.all_gather(residual[None].astype(jnp.bfloat16), 'tm', axis=0, tiled=T...  112 us
    ppermute x39, starting transfers between devices, with_halo(): lax.ppermute(head, axis, [((i + 1) % count, i) for i in range(count)])  100 us
  transfers between devices with their start and end apart: 84, of which 45 were waited for; matrix products, arithmetic and copies ran while one was open for 0% of the time, Pallas kernels for 0%

commit v1 on v0

v1 whole, which is shorter than its diff:
```python
import functools

import jax
import jax.numpy as jnp
from jax import lax
from jax.experimental import pallas as pl
from jax.experimental.pallas import tpu as pltpu
from jax.sharding import PartitionSpec as P

F32, BF16 = jnp.float32, jnp.bfloat16
MESH = pl.DeviceIdType.MESH

STEPS = 8
NTM = 32
SLAB = 48
NY = 512
LANES = 128
GROUPS = NY // LANES
OWNERS = 12
ROWS = SLAB // OWNERS
TILE = ROWS * GROUPS
OUTER = 16
INNER = 8


def owner_of(chunk):
    return 8 + chunk + (2 if chunk >= OWNERS // 2 else 0)


def split(x):
    high = x.astype(BF16)
    return high, (x - high.astype(F32)).astype(BF16)


def dot(a, b):
    return jnp.dot(a, b, preferred_element_type=F32)


def dot3(x, high, low):
    rows = x.shape[0]
    xh, xl = split(x)
    both = dot(jnp.concatenate([xh, xl], axis=0), high)
    return both[:rows] + both[rows:] + dot(xh, low)


def kernel(u0_hbm, vel_hbm, dif_hbm, forcing_hbm, imp_hbm, coarse_hbm, out,
           mv, cv, mh, ml, cl, pw, plow, ptmp, fin, vin, din, uin, fpack, fhalo,
           wext, fext, bsend, brecv, dsend, drecv, flat, fwd_send, fwd_recv, flat2,
           back1_send, back1_recv, flat3, back2_send, back2_recv, chold,
           in_sem, halo_send, halo_recv, u_send, u_recv, sh_send, sh_recv,
           fs_sem, fr_sem, bks_sem, bkr_sem):
    p = lax.axis_index("tm")
    s = lax.axis_index("space")
    nsp = lax.axis_size("space")
    up = lax.rem(s + nsp - 1, nsp)
    down = lax.rem(s + 1, nsp)
    first = p == 0
    is_owner = ((p >= 8) & (p < 14)) | ((p >= 16) & (p < 22))
    chunk = jnp.where(p < 14, p - 8, p - 10)
    top_owner = is_owner & (chunk < 4)
    bottom_owner = is_owner & (chunk >= OWNERS - 4)
    top2_owner = is_owner & (chunk < 2)
    bottom2_owner = is_owner & (chunk >= OWNERS - 2)

    barrier = pltpu.get_barrier_semaphore()

    def greet(tm, space):
        pl.semaphore_signal(barrier, inc=1, device_id=(tm, space), device_id_type=MESH)

    greet(p, up)
    greet(p, down)

    @pl.when(p < NTM - 1)
    def _():
        for other in (up, s, down):
            greet(p + 1, other)

    @pl.when(p > 0)
    def _():
        for other in (up, s, down):
            greet(p - 1, other)

    for j in range(OWNERS):
        @pl.when(p != owner_of(j))
        def _():
            greet(owner_of(j), s)
        if j < 4:
            greet(owner_of(j), down)
        if j >= OWNERS - 4:
            greet(owner_of(j), up)

    @pl.when(is_owner)
    def _():
        @pl.loop(1, NTM)
        def _(i):
            greet(lax.rem(p + i, NTM), s)

    @pl.when(top_owner)
    def _():
        @pl.loop(0, NTM)
        def _(i):
            greet(i, up)

    @pl.when(bottom_owner)
    def _():
        @pl.loop(0, NTM)
        def _(i):
            greet(i, down)

    loads = [
        pltpu.make_async_copy(forcing_hbm, fin, in_sem.at[0]),
        pltpu.make_async_copy(imp_hbm, mv, in_sem.at[1]),
        pltpu.make_async_copy(vel_hbm, vin.at[pl.ds(OUTER, SLAB)], in_sem.at[2]),
        pltpu.make_async_copy(dif_hbm, din.at[pl.ds(OUTER, SLAB)], in_sem.at[3]),
        pltpu.make_async_copy(u0_hbm, uin.at[pl.ds(INNER, SLAB)], in_sem.at[4]),
        pltpu.make_async_copy(coarse_hbm, cv, in_sem.at[5]),
    ]
    for load in loads:
        load.start()

    loads[0].wait()
    sub = lax.broadcasted_iota(jnp.int32, (INNER, NY), 0)
    lower = [fin[k, SLAB - 16:SLAB, :].astype(F32)[8:] for k in range(7)]
    upper = [fin[k, 0:16, :].astype(F32)[:8] for k in range(7)]
    for side, rows in ((0, lower), (1, upper)):
        packed = []
        for k in range(4):
            if k == 3:
                packed.append(rows[3])
                continue
            count = k + 1
            if side == 0:
                moved = pltpu.roll(rows[6 - k], count, 0)
                packed.append(jnp.where(sub < count, moved, rows[k]))
            else:
                moved = pltpu.roll(rows[6 - k], INNER - count, 0)
                packed.append(jnp.where(sub >= INNER - count, moved, rows[k]))
        fpack[side] = jnp.concatenate(packed, axis=0).astype(BF16)

    total = (2 + 12 + 8 + jnp.where(p < NTM - 1, 3, 0) + jnp.where(p > 0, 3, 0)
             + jnp.where(is_owner, NTM - 2, 0)
             + jnp.where(top_owner, NTM, 0) + jnp.where(bottom_owner, NTM, 0))
    pl.semaphore_wait(barrier, total)

    def remote(src, dst, send, recv, tm, space):
        return pltpu.make_async_remote_copy(src_ref=src, dst_ref=dst, send_sem=send, recv_sem=recv,
                                            device_id=(tm, space), device_id_type=MESH)

    edge_low, edge_high = pl.ds(0, OUTER), pl.ds(OUTER + SLAB, OUTER)
    own_low, own_high = pl.ds(0, 16), pl.ds(SLAB - 16, 16)
    halos = [
        remote(fpack.at[0], fhalo.at[0], halo_send.at[0], halo_recv.at[0], p, down),
        remote(fpack.at[1], fhalo.at[1], halo_send.at[1], halo_recv.at[1], p, up),
        remote(vel_hbm.at[own_high], vin.at[edge_low], halo_send.at[2], halo_recv.at[2], p, down),
        remote(vel_hbm.at[own_low], vin.at[edge_high], halo_send.at[3], halo_recv.at[3], p, up),
        remote(dif_hbm.at[own_high], din.at[edge_low], halo_send.at[4], halo_recv.at[4], p, down),
        remote(dif_hbm.at[own_low], din.at[edge_high], halo_send.at[5], halo_recv.at[5], p, up),
    ]
    for copy in halos:
        copy.start()
    u_halos = [
        remote(u0_hbm.at[pl.ds(SLAB - INNER, INNER)], uin.at[pl.ds(0, INNER)], u_send.at[0], u_recv.at[0], p, down),
        remote(u0_hbm.at[pl.ds(0, INNER)], uin.at[pl.ds(INNER + SLAB, INNER)], u_send.at[1], u_recv.at[1], p, up),
    ]

    @pl.when(first)
    def _():
        for copy in u_halos:
            copy.start()

    loads[1].wait()
    a, b = split(mv[...])
    mh[...] = a
    ml[...] = b
    loads[5].wait()
    a, b = split(cv[...])
    pw[0] = a
    cl[...] = b
    plow[...] = b
    for k in range(STEPS):
        fext[k, INNER:INNER + SLAB, :] = fin[k].astype(F32)

    def square(k):
        @pl.loop(0, 4)
        def _(i):
            rows = pl.ds(pl.multiple_of(i * 128, 128), 128)
            xh, xl = pw[k - 1, rows, :], plow[rows, :]
            both = dot(jnp.concatenate([xh, xl], axis=0), pw[k - 1])
            ptmp[rows, :] = both[:128] + both[128:] + dot(xh, plow[...])

        high, low = split(ptmp[...])
        pw[k] = high
        plow[...] = low

    @pl.when(is_owner)
    def _():
        square(1)
        square(2)

    for load in loads[2:5]:
        load.wait()
    for copy in halos:
        copy.wait_recv()

    spread = din[...].astype(F32)
    half = 0.5 * vin[...].astype(F32)
    wext[0] = spread + half
    wext[1] = 1.0 - 2.0 * spread
    wext[2] = spread - half
    for side, at in ((0, 0), (1, INNER + SLAB)):
        packed = fhalo[side].astype(F32)
        for k in range(STEPS):
            if k < 4:
                rows = packed[8 * k:8 * k + 8]
            elif k < 7:
                rows = packed[8 * (6 - k):8 * (7 - k)]
                rows = pltpu.roll(rows, INNER - (7 - k) if side == 0 else 7 - k, 0)
            else:
                rows = jnp.zeros((INNER, NY), F32)
            fext[k, at:at + INNER, :] = rows

    @pl.when(first)
    def _():
        for copy in u_halos:
            copy.wait_recv()

    def advance(v, weights, forced):
        west, centre, east = weights
        rows = v.shape[0]
        mixed = centre * v + east * pltpu.roll(v, rows - 1, 0) + west * pltpu.roll(v, 1, 0)
        if forced is not None:
            mixed = mixed + forced
        return dot3(mixed, mh[...], ml[...])

    def weights64():
        return tuple(wext[i, 8:72, :] for i in range(3))

    def sweep(v, weights, forced):
        def turn(k, v):
            return advance(v, weights(), fext[k] if forced else None)
        return lax.fori_loop(0, STEPS, turn, v)

    def weights128():
        return tuple(jnp.concatenate([w, w], axis=0) for w in weights64())

    def weights80():
        return tuple(wext[i] for i in range(3))

    def shift(src, dst, at):
        return [
            remote(src, dst.at[pl.ds(INNER, SLAB)], sh_send.at[at], sh_recv.at[at], p + 1, s),
            remote(src.at[pl.ds(0, INNER)], dst.at[pl.ds(INNER + SLAB, INNER)],
                   sh_send.at[at + 1], sh_recv.at[at + 1], p + 1, up),
            remote(src.at[pl.ds(SLAB - INNER, INNER)], dst.at[pl.ds(0, INNER)],
                   sh_send.at[at + 2], sh_recv.at[at + 2], p + 1, down),
        ]

    def start_shift(copies):
        @pl.when(p < NTM - 1)
        def _():
            for copy in copies:
                copy.start()

    def end_shift(copies, dst):
        @pl.when(p > 0)
        def _():
            for copy in copies:
                copy.wait_recv()

        @pl.when(first)
        def _():
            dst[...] = jnp.zeros_like(dst)

    begin = jnp.where(first, uin[...], jnp.zeros((64, NY), F32))
    bsend[...] = sweep(begin, weights64, True)[8:56]
    b_copies = shift(bsend, brecv, 0)
    start_shift(b_copies)

    @pl.when(is_owner)
    def _():
        square(3)
        square(4)

    end_shift(b_copies, brecv)
    dsend[...] = sweep(brecv[...], weights64, False)[8:56]
    d_copies = shift(dsend, drecv, 3)

    def forward(which, rows):
        for g in range(GROUPS):
            flat[pl.ds(g, SLAB, stride=GROUPS), :] = rows[:, g * LANES:(g + 1) * LANES]
        fwd_send[which] = flat[...].astype(BF16)
        mine = pl.ds(pl.multiple_of(p * TILE, TILE), TILE)
        for j in range(OWNERS):
            part = pl.ds(j * TILE, TILE)
            copy = remote(fwd_send.at[which, part], fwd_recv.at[which, mine],
                          fs_sem.at[which], fr_sem.at[which], owner_of(j), s)

            @pl.when(p != owner_of(j))
            def _():
                copy.start()

            @pl.when(p == owner_of(j))
            def _():
                fwd_recv[which, mine, :] = fwd_send[which, part, :]

    def forward_end(which):
        def wait(n):
            remote(fwd_send.at[which, pl.ds(0, n * TILE)], fwd_recv.at[which, pl.ds(0, n * TILE)],
                   fs_sem.at[which], fr_sem.at[which], p, up).wait_send()

        @pl.when(is_owner)
        def _():
            wait(OWNERS - 1)

        @pl.when(jnp.logical_not(is_owner))
        def _():
            wait(OWNERS)

    def scan(which, delay, result):
        count = (NTM - 1) * TILE
        remote(fwd_recv.at[which, pl.ds(0, count)], fwd_recv.at[which, pl.ds(0, count)],
               fs_sem.at[which], fr_sem.at[which], p, up).wait_recv()
        flat2[...] = fwd_recv[which].astype(F32)
        size = NTM * ROWS
        total = jnp.concatenate([flat2[pl.ds(g, size, stride=GROUPS), :] for g in range(GROUPS)], axis=1)
        row = lax.broadcasted_iota(jnp.int32, (size, NY), 0)

        def later(x, blocks):
            return jnp.where(row >= blocks * ROWS, pltpu.roll(x, blocks * ROWS, 0), 0.0)

        total = later(total, delay)
        for k in range(5):
            total = total + dot(later(total, 1 << k).astype(BF16), pw[k])
        for g in range(GROUPS):
            flat2[pl.ds(g, size, stride=GROUPS), :] = total[:, g * LANES:(g + 1) * LANES]
        result[...] = flat2[...].astype(result.dtype)

    def back(which, src, dst, edge, top, bottom):
        def copy(block, place, space):
            return remote(src.at[pl.ds(pl.multiple_of(block * TILE, TILE), TILE)],
                          dst.at[pl.ds(pl.multiple_of(place * TILE, TILE), TILE)],
                          bks_sem.at[which], bkr_sem.at[which], block, space)

        @pl.when(top)
        def _():
            @pl.loop(0, NTM)
            def _(i):
                copy(i, edge + OWNERS + chunk, up).start()

        @pl.when(bottom)
        def _():
            @pl.loop(0, NTM)
            def _(i):
                copy(i, chunk - (OWNERS - edge), down).start()

        @pl.loop(1, NTM)
        def _(i):
            copy(lax.rem(p + i, NTM), edge + chunk, s).start()

        at = pl.ds(pl.multiple_of((edge + chunk) * TILE, TILE), TILE)
        dst[at, :] = src[pl.ds(pl.multiple_of(p * TILE, TILE), TILE), :]

    def back_wait(which, dst, edge):
        def wait(n):
            part = dst.at[pl.ds(0, n * TILE)]
            remote(part, part, bks_sem.at[which], bkr_sem.at[which], p, up).wait_recv()

        @pl.when(is_owner)
        def _():
            wait(OWNERS + 2 * edge - 1)

        @pl.when(jnp.logical_not(is_owner))
        def _():
            wait(OWNERS + 2 * edge)

    def back_end(which, src, on_edge):
        def wait(n):
            part = src.at[pl.ds(0, n * TILE)]
            remote(part, part, bks_sem.at[which], bkr_sem.at[which], p, up).wait_send()

        @pl.when(is_owner)
        def _():
            wait(NTM - 1)

        @pl.when(on_edge)
        def _():
            wait(NTM)

    forward(0, dsend[...])
    start_shift(d_copies)

    @pl.when(is_owner)
    def _():
        scan(0, 2, back1_send)
        back(0, back1_send, back1_recv, 4, top_owner, bottom_owner)

    back_wait(0, back1_recv, 4)
    flat3[...] = back1_recv[...].astype(F32)
    before = jnp.concatenate([flat3[pl.ds(g, 80, stride=GROUPS), :] for g in range(GROUPS)], axis=1)
    chold[...] = before

    previous_w = sweep(before, weights80, False)[8:72]
    end_shift(d_copies, drecv)
    carried = dot3(chold[8:72, :], pw[0], cl[...])
    pair = jnp.concatenate([previous_w - carried, drecv[...] + carried], axis=0)
    drecv[...] = brecv[...] + drecv[...] + previous_w
    pair = sweep(pair, weights128, False)
    residual = pair[8:56]
    forward(1, residual)
    out[7] = bsend[...] + dsend[...] + pair[72:120] + residual

    @pl.when(is_owner)
    def _():
        scan(1, 1, back2_send)
        back(1, back2_send, back2_recv, 2, top2_owner, bottom2_owner)

    back_wait(1, back2_recv, 2)
    correction = jnp.concatenate([back2_recv[pl.ds(g, 64, stride=GROUPS), :] for g in range(GROUPS)], axis=1)
    v = jnp.where(first, uin[...], drecv[...] + correction)
    out[7] = out[7] + dot3(correction[8:56], pw[0], cl[...])

    def last(k, v):
        v = advance(v, weights64(), fext[k])
        out[k] = v[8:56]
        return v

    lax.fori_loop(0, STEPS - 1, last, v)

    for sent in halos:
        sent.wait_send()

    @pl.when(first)
    def _():
        for sent in u_halos:
            sent.wait_send()

    @pl.when(p < NTM - 1)
    def _():
        for sent in b_copies + d_copies:
            sent.wait_send()

    forward_end(0)
    forward_end(1)
    back_end(0, back1_send, top_owner | bottom_owner)
    back_end(1, back2_send, top2_owner | bottom2_owner)


def per_device(initial_state, velocity, diffusion, forcing, implicit, coarse_implicit):
    V = pltpu.VMEM
    DMA = pltpu.SemaphoreType.DMA
    square = (NY, NY)
    scratch = [
        V(square, F32), V(square, F32), V(square, BF16), V(square, BF16), V(square, BF16),
        V((5,) + square, BF16), V(square, BF16), V(square, F32),
        V((STEPS, SLAB, NY), BF16), V((80, NY), BF16), V((80, NY), BF16), V((64, NY), F32),
        V((2, 32, NY), BF16), V((2, 32, NY), BF16),
        V((3, 80, NY), F32), V((STEPS, 64, NY), F32),
        V((SLAB, NY), F32), V((64, NY), F32), V((SLAB, NY), F32), V((64, NY), F32),
        V((SLAB * GROUPS, LANES), F32), V((2, SLAB * GROUPS, LANES), BF16),
        V((2, NTM * TILE, LANES), BF16), V((NTM * TILE, LANES), F32),
        V((NTM * TILE, LANES), BF16), V((80 * GROUPS, LANES), BF16), V((80 * GROUPS, LANES), F32),
        V((NTM * TILE, LANES), F32), V((64 * GROUPS, LANES), F32), V((80, NY), F32),
        DMA((6,)), DMA((6,)), DMA((6,)), DMA((2,)), DMA((2,)), DMA((6,)), DMA((6,)),
        DMA((2,)), DMA((2,)), DMA((2,)), DMA((2,)),
    ]
    return pl.pallas_call(
        kernel,
        out_shape=jax.ShapeDtypeStruct((STEPS, SLAB, NY), F32),
        in_specs=[pl.BlockSpec(memory_space=pl.ANY)] * 6,
        out_specs=pl.BlockSpec(memory_space=pltpu.VMEM),
        scratch_shapes=scratch,
        compiler_params=pltpu.CompilerParams(
            collective_id=0, has_side_effects=True, vmem_limit_bytes=40 * 2**20),
    )(initial_state, velocity, diffusion, forcing, implicit, coarse_implicit)


def solution(mesh):
    in_specs = (
        P("space", None),
        P("space", None),
        P("space", None),
        P("tm", "space", None),
        P(),
        P(),
    )
    return jax.shard_map(
        per_device, mesh=mesh, in_specs=in_specs, out_specs=P("tm", "space", None), check_vma=False
    )
```

time: 859 us -> 84.8 us (0.10)
  the two profiles are of different devices: /device:TPU:102 before, /device:TPU:1 now
where the time goes in v1:
time: 84.8 us; the launch traced here: 84.5 us
  Pallas kernels  77.7 us (92%)
  local copies, waits for them, and re-layouts  6.81 us (8%)
    pallas_call x1, Pallas kernels, per_device(): pl.pallas_call(kernel, out_shape=jax.ShapeDtypeStruct((STEPS, SLAB, NY),...  77.7 us
    unnamed x13, local copies, waits for them, and re-layouts  6.81 us

profile of v1, /device:TPU:1, one launch (start us, length us, event | category | flops | bytes accessed | tf_op | source)
XLA Modules:
  0.0 84.5 jit_solution(14027447014323418274)
XLA Ops:
  0.0 0.0 copy-start
  0.0 1.2 %copy-done = f32[512,512]{1,0:T(8,128)S(1)} copy-done((f32[512,512]{1,0:T(8,128)S(1)}, f32[512,512]{1,0:T(8,128)}, u32[]{:S(2)}) %copy-start) | copy-done | bytes 1048600
  1.2 0.0 copy-start.1
  1.2 1.2 %copy-done.1 = f32[512,512]{1,0:T(8,128)S(1)} copy-done((f32[512,512]{1,0:T(8,128)S(1)}, f32[512,512]{1,0:T(8,128)}, u32[]{:S(2)}) %copy-start.1) | copy-done | bytes 1048600
  2.5 0.0 copy-start.2
  2.5 1.0 %copy-done.2 = bf16[8,48,512]{2,1,0:T(8,128)(2,1)S(1)} copy-done((bf16[8,48,512]{2,1,0:T(8,128)(2,1)S(1)}, bf16[8,48,512]{2,1,0:T(8,128)(2,1)}, u32[]{:S(2)}) %copy-start.2) | copy-done | bytes 393240
  3.4 0.0 copy-start.3
  3.4 0.9 %copy-done.3 = f32[48,512]{1,0:T(8,128)S(1)} copy-done((f32[48,512]{1,0:T(8,128)S(1)}, f32[48,512]{1,0:T(8,128)}, u32[]{:S(2)}) %copy-start.3) | copy-done | bytes 98328
  4.3 0.0 copy-start.4
  4.3 0.8 copy-done.4
  5.1 0.0 copy-start.5
  5.1 0.8 copy-done.5
  5.9 77.7 %shard_map.64 = f32[8,48,512]{2,1,0:T(8,128)S(1)} custom-call(f32[48,512]{1,0:T(8,128)S(1)} %copy-done.3, bf16[48,512]{1,0:T(8,128)(2,1)S(1)} %copy-done.4, bf16[48,512]{1,0:T(8,128)(2,1)S(1)} %copy-done.5, bf16[8,48,512]{2,1,0:T(8,128)(2,1)S(1)} %copy-done.2, f32[512,512]{1,0:T(8,128)S(1)} %copy-done, f32[512,512]{1,0:T(8,128)S(1)} %copy-done.1), custom_call_target="tpu_custom_call" | custom-call | tf_op jit(solution)/shard_map/pallas_call | solution.py:466
  83.6 0.9 %copy.8 = f32[8,48,512]{2,1,0:T(8,128)} copy(f32[8,48,512]{2,1,0:T(8,128)S(1)} %shard_map.64) | data formatting | bytes 1572864
Async XLA Ops:
  0.0 1.2 %copy-start = (f32[512,512]{1,0:T(8,128)S(1)}, f32[512,512]{1,0:T(8,128)}, u32[]{:S(2)}) copy-start(f32[512,512]{1,0:T(8,128)} %imp_hbm.1) | copy-start | bytes 3145732
  1.2 1.2 %copy-start.1 = (f32[512,512]{1,0:T(8,128)S(1)}, f32[512,512]{1,0:T(8,128)}, u32[]{:S(2)}) copy-start(f32[512,512]{1,0:T(8,128)} %coarse_hbm.1) | copy-start | bytes 3145732
  2.5 1.0 %copy-start.2 = (bf16[8,48,512]{2,1,0:T(8,128)(2,1)S(1)}, bf16[8,48,512]{2,1,0:T(8,128)(2,1)}, u32[]{:S(2)}) copy-start(bf16[8,48,512]{2,1,0:T(8,128)(2,1)} %forcing_hbm.1) | copy-start | bytes 1179652
  3.4 0.9 %copy-start.3 = (f32[48,512]{1,0:T(8,128)S(1)}, f32[48,512]{1,0:T(8,128)}, u32[]{:S(2)}) copy-start(f32[48,512]{1,0:T(8,128)} %u0_hbm.1) | copy-start | bytes 294916
  4.3 0.8 copy-start.4
  5.1 0.8 copy-start.5

commit v2 on v1

--- a/solution.py
+++ b/solution.py
@@ -23,8 +23,11 @@
 INNER = 8
 
 
+OWNER_OF = (8, 10, 12, 14, 9, 13, 19, 23, 16, 18, 20, 22)
+
+
 def owner_of(chunk):
-    return 8 + chunk + (2 if chunk >= OWNERS // 2 else 0)
+    return OWNER_OF[chunk]
 
 
 def split(x):
@@ -55,57 +58,14 @@
     up = lax.rem(s + nsp - 1, nsp)
     down = lax.rem(s + 1, nsp)
     first = p == 0
-    is_owner = ((p >= 8) & (p < 14)) | ((p >= 16) & (p < 22))
-    chunk = jnp.where(p < 14, p - 8, p - 10)
+    chunk = jnp.int32(-1)
+    for j in range(OWNERS):
+        chunk = jnp.where(p == OWNER_OF[j], j, chunk)
+    is_owner = chunk >= 0
     top_owner = is_owner & (chunk < 4)
     bottom_owner = is_owner & (chunk >= OWNERS - 4)
     top2_owner = is_owner & (chunk < 2)
     bottom2_owner = is_owner & (chunk >= OWNERS - 2)
-
-    barrier = pltpu.get_barrier_semaphore()
-
-    def greet(tm, space):
-        pl.semaphore_signal(barrier, inc=1, device_id=(tm, space), device_id_type=MESH)
-
-    greet(p, up)
-    greet(p, down)
-
-    @pl.when(p < NTM - 1)
-    def _():
-        for other in (up, s, down):
-            greet(p + 1, other)
-
-    @pl.when(p > 0)
-    def _():
-        for other in (up, s, down):
-            greet(p - 1, other)
-
-    for j in range(OWNERS):
-        @pl.when(p != owner_of(j))
-        def _():
-            greet(owner_of(j), s)
-        if j < 4:
-            greet(owner_of(j), down)
-        if j >= OWNERS - 4:
-            greet(owner_of(j), up)
-
-    @pl.when(is_owner)
-    def _():
-        @pl.loop(1, NTM)
-        def _(i):
-            greet(lax.rem(p + i, NTM), s)
-
-    @pl.when(top_owner)
-    def _():
-        @pl.loop(0, NTM)
-        def _(i):
-            greet(i, up)
-
-    @pl.when(bottom_owner)
-    def _():
-        @pl.loop(0, NTM)
-        def _(i):
-            greet(i, down)
 
     loads = [
         pltpu.make_async_copy(forcing_hbm, fin, in_sem.at[0]),
@@ -117,6 +77,82 @@
     ]
     for load in loads:
         load.start()
+
+    barrier = pltpu.get_barrier_semaphore()
+
+    def greet(tm, space):
+        pl.semaphore_signal(barrier, inc=1, device_id=(tm, space), device_id_type=MESH)
+
+    greet(p, up)
+    greet(p, down)
+
+    @pl.when(p < NTM - 1)
+    def _():
+        for other in (up, s, down):
+            greet(p + 1, other)
+
+    @pl.when(p > 0)
+    def _():
+        for other in (up, s, down):
+            greet(p - 1, other)
+
+    for j in range(OWNERS):
+        @pl.when(p != owner_of(j))
+        def _():
+            greet(owner_of(j), s)
+        if j < 4:
+            greet(owner_of(j), down)
+        if j >= OWNERS - 4:
+            greet(owner_of(j), up)
+
+    @pl.when(is_owner)
+    def _():
+        @pl.loop(1, NTM)
+        def _(i):
+            greet(lax.rem(p + i, NTM), s)
+
+    @pl.when(top_owner)
+    def _():
+        @pl.loop(0, NTM)
+        def _(i):
+            greet(i, up)
+
+    @pl.when(bottom_owner)
+    def _():
+        @pl.loop(0, NTM)
+        def _(i):
+            greet(i, down)
+
+    total = (2 + 12 + 8 + jnp.where(p < NTM - 1, 3, 0) + jnp.where(p > 0, 3, 0)
+             + jnp.where(is_owner, NTM - 2, 0)
+             + jnp.where(top_owner, NTM, 0) + jnp.where(bottom_owner, NTM, 0))
+    pl.semaphore_wait(barrier, total)
+
+    def remote(src, dst, send, recv, tm, space):
+        return pltpu.make_async_remote_copy(src_ref=src, dst_ref=dst, send_sem=send, recv_sem=recv,
+                                            device_id=(tm, space), device_id_type=MESH)
+
+    edge_low, edge_high = pl.ds(0, OUTER), pl.ds(OUTER + SLAB, OUTER)
+    own_low, own_high = pl.ds(0, 16), pl.ds(SLAB - 16, 16)
+    halos = [
+        remote(fpack.at[0], fhalo.at[0], halo_send.at[0], halo_recv.at[0], p, down),
+        remote(fpack.at[1], fhalo.at[1], halo_send.at[1], halo_recv.at[1], p, up),
+        remote(vel_hbm.at[own_high], vin.at[edge_low], halo_send.at[2], halo_recv.at[2], p, down),
+        remote(vel_hbm.at[own_low], vin.at[edge_high], halo_send.at[3], halo_recv.at[3], p, up),
+        remote(dif_hbm.at[own_high], din.at[edge_low], halo_send.at[4], halo_recv.at[4], p, down),
+        remote(dif_hbm.at[own_low], din.at[edge_high], halo_send.at[5], halo_recv.at[5], p, up),
+    ]
+    for copy in halos[2:]:
+        copy.start()
+    u_halos = [
+        remote(u0_hbm.at[pl.ds(SLAB - INNER, INNER)], uin.at[pl.ds(0, INNER)], u_send.at[0], u_recv.at[0], p, down),
+        remote(u0_hbm.at[pl.ds(0, INNER)], uin.at[pl.ds(INNER + SLAB, INNER)], u_send.at[1], u_recv.at[1], p, up),
+    ]
+
+    @pl.when(first)
+    def _():
+        for copy in u_halos:
+            copy.start()
 
     loads[0].wait()
     sub = lax.broadcasted_iota(jnp.int32, (INNER, NY), 0)
@@ -137,36 +173,8 @@
                 packed.append(jnp.where(sub >= INNER - count, moved, rows[k]))
         fpack[side] = jnp.concatenate(packed, axis=0).astype(BF16)
 
-    total = (2 + 12 + 8 + jnp.where(p < NTM - 1, 3, 0) + jnp.where(p > 0, 3, 0)
-             + jnp.where(is_owner, NTM - 2, 0)
-             + jnp.where(top_owner, NTM, 0) + jnp.where(bottom_owner, NTM, 0))
-    pl.semaphore_wait(barrier, total)
-
-    def remote(src, dst, send, recv, tm, space):
-        return pltpu.make_async_remote_copy(src_ref=src, dst_ref=dst, send_sem=send, recv_sem=recv,
-                                            device_id=(tm, space), device_id_type=MESH)
-
-    edge_low, edge_high = pl.ds(0, OUTER), pl.ds(OUTER + SLAB, OUTER)
-    own_low, own_high = pl.ds(0, 16), pl.ds(SLAB - 16, 16)
-    halos = [
-        remote(fpack.at[0], fhalo.at[0], halo_send.at[0], halo_recv.at[0], p, down),
-        remote(fpack.at[1], fhalo.at[1], halo_send.at[1], halo_recv.at[1], p, up),
-        remote(vel_hbm.at[own_high], vin.at[edge_low], halo_send.at[2], halo_recv.at[2], p, down),
-        remote(vel_hbm.at[own_low], vin.at[edge_high], halo_send.at[3], halo_recv.at[3], p, up),
-        remote(dif_hbm.at[own_high], din.at[edge_low], halo_send.at[4], halo_recv.at[4], p, down),
-        remote(dif_hbm.at[own_low], din.at[edge_high], halo_send.at[5], halo_recv.at[5], p, up),
-    ]
-    for copy in halos:
+    for copy in halos[:2]:
         copy.start()
-    u_halos = [
-        remote(u0_hbm.at[pl.ds(SLAB - INNER, INNER)], uin.at[pl.ds(0, INNER)], u_send.at[0], u_recv.at[0], p, down),
-        remote(u0_hbm.at[pl.ds(0, INNER)], uin.at[pl.ds(INNER + SLAB, INNER)], u_send.at[1], u_recv.at[1], p, up),
-    ]
-
-    @pl.when(first)
-    def _():
-        for copy in u_halos:
-            copy.start()
 
     loads[1].wait()
     a, b = split(mv[...])
@@ -471,7 +479,8 @@
         scratch_shapes=scratch,
         compiler_params=pltpu.CompilerParams(
             collective_id=0, has_side_effects=True, vmem_limit_bytes=40 * 2**20),
-    )(initial_state, velocity, diffusion, forcing, implicit, coarse_implicit)
+    )(*[pltpu.with_memory_space_constraint(x, pltpu.HBM)
+        for x in (initial_state, velocity, diffusion, forcing, implicit, coarse_implicit)])
 
 
 def solution(mesh):

time: 84.8 us -> 75.6 us (0.89); the launches traced: 84.5 us -> 74.4 us
  local copies, waits for them, and re-layouts: 6.81 us -> 0.88 us
  Pallas kernels: 77.7 us -> 73.5 us
    unnamed x13 -> x1, local copies, waits for them, and re-layouts: 6.81 us -> 0.88 us
    pallas_call x1, Pallas kernels: 77.7 us -> 73.5 us  [per_device(): pl.pallas_call(kernel, out_shape=jax.ShapeDtypeStruct((STEPS, SLAB, NY),...]
where the time goes in v2:
time: 75.6 us; the launch traced here: 74.4 us
  Pallas kernels  73.5 us (97%)
  local copies, waits for them, and re-layouts  0.88 us (1%)
    pallas_call x1, Pallas kernels, per_device(): pl.pallas_call(kernel, out_shape=jax.ShapeDtypeStruct((STEPS, SLAB, NY),...  73.5 us

profile of v2, /device:TPU:1, one launch (start us, length us, event | category | flops | bytes accessed | tf_op | source)
XLA Modules:
  0.0 74.4 jit_solution(13042455245788167004)
XLA Ops:
  0.0 73.5 %shard_map.64 = f32[8,48,512]{2,1,0:T(8,128)S(1)} custom-call(f32[48,512]{1,0:T(8,128)} %u0_hbm.1, bf16[48,512]{1,0:T(8,128)(2,1)} %vel_hbm.1, bf16[48,512]{1,0:T(8,128)(2,1)} %dif_hbm.1, bf16[8,48,512]{2,1,0:T(8,128)(2,1)} %forcing_hbm.1, f32[512,512]{1,0:T(8,128)} %imp_hbm.1, f32[512,512]{1,0:T(8,128)} %coarse_hbm.1), custom_call_target="tpu_custom_call" | custom-call | tf_op jit(solution)/shard_map/pallas_call | solution.py:474
  73.5 0.9 %copy.8 = f32[8,48,512]{2,1,0:T(8,128)} copy(f32[8,48,512]{2,1,0:T(8,128)S(1)} %shard_map.64) | data formatting | bytes 1572864

commit v3 on v2

v3 whole, which is shorter than its diff:
```python
import functools

import jax
import jax.numpy as jnp
from jax import lax
from jax.experimental import pallas as pl
from jax.experimental.pallas import tpu as pltpu
from jax.sharding import PartitionSpec as P

F32, BF16 = jnp.float32, jnp.bfloat16
MESH = pl.DeviceIdType.MESH

STEPS = 8
NTM = 32
SLAB = 48
NY = 512
LANES = 128
GROUPS = NY // LANES
OWNERS = 12
ROWS = SLAB // OWNERS
TILE = ROWS * GROUPS
OUTER = 16
INNER = 8


OWNER_OF = (8, 10, 12, 14, 9, 13, 19, 23, 16, 18, 20, 22)


def owner_of(chunk):
    return OWNER_OF[chunk]


def split(x):
    high = x.astype(BF16)
    return high, (x - high.astype(F32)).astype(BF16)


def dot(a, b):
    return jnp.dot(a, b, preferred_element_type=F32)


def dot3(x, high, low):
    rows = x.shape[0]
    xh, xl = split(x)
    both = dot(jnp.concatenate([xh, xl], axis=0), high)
    return both[:rows] + both[rows:] + dot(xh, low)


def kernel(u0_hbm, vel_hbm, dif_hbm, forcing_hbm, imp_hbm, coarse_hbm, out,
           mv, cv, mh, ml, cl, pw, plow, ptmp, fin, vin, din, uin, fpack, fhalo,
           wext, fext, fprev, bsend, brecv, dsend, drecv, flat, fwd_send, fwd_recv, flat2,
           back1_send, back1_recv, flat3, back2_send, back2_recv, chold, carry,
           in_sem, halo_send, halo_recv, u_send, u_recv, sh_send, sh_recv,
           fs_sem, fr_sem, bks_sem, bkr_sem):
    p = lax.axis_index("tm")
    s = lax.axis_index("space")
    nsp = lax.axis_size("space")
    up = lax.rem(s + nsp - 1, nsp)
    down = lax.rem(s + 1, nsp)
    first = p == 0
    starts = p < 2
    chunk = jnp.int32(-1)
    for j in range(OWNERS):
        chunk = jnp.where(p == OWNER_OF[j], j, chunk)
    is_owner = chunk >= 0
    top_owner = is_owner & (chunk < 4)
    bottom_owner = is_owner & (chunk >= OWNERS - 4)
    top2_owner = is_owner & (chunk < 2)
    bottom2_owner = is_owner & (chunk >= OWNERS - 2)

    loads = [
        pltpu.make_async_copy(forcing_hbm, fin, in_sem.at[0]),
        pltpu.make_async_copy(imp_hbm, mv, in_sem.at[1]),
        pltpu.make_async_copy(vel_hbm, vin.at[pl.ds(OUTER, SLAB)], in_sem.at[2]),
        pltpu.make_async_copy(dif_hbm, din.at[pl.ds(OUTER, SLAB)], in_sem.at[3]),
        pltpu.make_async_copy(u0_hbm, uin.at[pl.ds(OUTER, SLAB)], in_sem.at[4]),
        pltpu.make_async_copy(coarse_hbm, cv, in_sem.at[5]),
    ]
    for load in loads:
        load.start()

    barrier = pltpu.get_barrier_semaphore()

    def greet(tm, space):
        pl.semaphore_signal(barrier, inc=1, device_id=(tm, space), device_id_type=MESH)

    greet(p, up)
    greet(p, down)

    @pl.when(p < NTM - 1)
    def _():
        for other in (up, s, down):
            greet(p + 1, other)

    @pl.when(p > 0)
    def _():
        for other in (up, s, down):
            greet(p - 1, other)

    for j in range(OWNERS):
        @pl.when(p != owner_of(j))
        def _():
            greet(owner_of(j), s)
        if j < 4:
            greet(owner_of(j), down)
        if j >= OWNERS - 4:
            greet(owner_of(j), up)

    @pl.when(is_owner)
    def _():
        @pl.loop(1, NTM)
        def _(i):
            greet(lax.rem(p + i, NTM), s)

    @pl.when(top_owner)
    def _():
        @pl.loop(0, NTM)
        def _(i):
            greet(i, up)

    @pl.when(bottom_owner)
    def _():
        @pl.loop(0, NTM)
        def _(i):
            greet(i, down)

    total = (2 + 12 + 8 + jnp.where(p < NTM - 1, 3, 0) + jnp.where(p > 0, 3, 0)
             + jnp.where(is_owner, NTM - 2, 0)
             + jnp.where(top_owner, NTM, 0) + jnp.where(bottom_owner, NTM, 0))
    pl.semaphore_wait(barrier, total)

    def remote(src, dst, send, recv, tm, space):
        return pltpu.make_async_remote_copy(src_ref=src, dst_ref=dst, send_sem=send, recv_sem=recv,
                                            device_id=(tm, space), device_id_type=MESH)

    edge_low, edge_high = pl.ds(0, OUTER), pl.ds(OUTER + SLAB, OUTER)
    own_low, own_high = pl.ds(0, 16), pl.ds(SLAB - 16, 16)
    halos = [
        remote(fpack.at[0], fhalo.at[0], halo_send.at[0], halo_recv.at[0], p, down),
        remote(fpack.at[1], fhalo.at[1], halo_send.at[1], halo_recv.at[1], p, up),
        remote(vel_hbm.at[own_high], vin.at[edge_low], halo_send.at[2], halo_recv.at[2], p, down),
        remote(vel_hbm.at[own_low], vin.at[edge_high], halo_send.at[3], halo_recv.at[3], p, up),
        remote(dif_hbm.at[own_high], din.at[edge_low], halo_send.at[4], halo_recv.at[4], p, down),
        remote(dif_hbm.at[own_low], din.at[edge_high], halo_send.at[5], halo_recv.at[5], p, up),
    ]
    u_halos = [
        remote(u0_hbm.at[own_high], uin.at[edge_low], u_send.at[0], u_recv.at[0], p, down),
        remote(u0_hbm.at[own_low], uin.at[edge_high], u_send.at[1], u_recv.at[1], p, up),
    ]

    half_steps = STEPS // 2
    ahead = []
    for at in range(2):
        steps = pl.ds(at * half_steps, half_steps)
        ahead += [
            remote(forcing_hbm.at[steps, own_low], fprev.at[steps, edge_high],
                   sh_send.at[3 * at], sh_recv.at[3 * at], p + 1, up),
            remote(forcing_hbm.at[steps, own_high], fprev.at[steps, edge_low],
                   sh_send.at[3 * at + 1], sh_recv.at[3 * at + 1], p + 1, down),
            remote(forcing_hbm.at[steps], fprev.at[steps, pl.ds(OUTER, SLAB)],
                   sh_send.at[3 * at + 2], sh_recv.at[3 * at + 2], p + 1, s),
        ]

    for copy in halos[2:]:
        copy.start()

    @pl.when(starts)
    def _():
        for copy in u_halos:
            copy.start()

    @pl.when(p < NTM - 1)
    def _():
        for copy in ahead:
            copy.start()

    @pl.when(first)
    def _():
        fprev[...] = jnp.zeros_like(fprev)

    loads[0].wait()
    sub = lax.broadcasted_iota(jnp.int32, (INNER, NY), 0)
    lower = [fin[k, SLAB - 16:SLAB, :].astype(F32)[8:] for k in range(7)]
    upper = [fin[k, 0:16, :].astype(F32)[:8] for k in range(7)]
    for side, rows in ((0, lower), (1, upper)):
        packed = []
        for k in range(4):
            if k == 3:
                packed.append(rows[3])
                continue
            count = k + 1
            if side == 0:
                moved = pltpu.roll(rows[6 - k], count, 0)
                packed.append(jnp.where(sub < count, moved, rows[k]))
            else:
                moved = pltpu.roll(rows[6 - k], INNER - count, 0)
                packed.append(jnp.where(sub >= INNER - count, moved, rows[k]))
        fpack[side] = jnp.concatenate(packed, axis=0).astype(BF16)

    for copy in halos[:2]:
        copy.start()

    loads[1].wait()
    a, b = split(mv[...])
    mh[...] = a
    ml[...] = b
    loads[5].wait()
    a, b = split(cv[...])
    pw[0] = a
    cl[...] = b
    plow[...] = b
    for k in range(STEPS):
        fext[k, INNER:INNER + SLAB, :] = fin[k].astype(F32)

    def square(k):
        @pl.loop(0, 4)
        def _(i):
            rows = pl.ds(pl.multiple_of(i * 128, 128), 128)
            xh, xl = pw[k - 1, rows, :], plow[rows, :]
            both = dot(jnp.concatenate([xh, xl], axis=0), pw[k - 1])
            ptmp[rows, :] = both[:128] + both[128:] + dot(xh, plow[...])

        high, low = split(ptmp[...])
        pw[k] = high
        plow[...] = low

    @pl.when(is_owner)
    def _():
        for k in range(1, 5):
            square(k)

    for load in loads[2:5]:
        load.wait()
    for copy in halos[2:]:
        copy.wait_recv()

    spread = din[...].astype(F32)
    half = 0.5 * vin[...].astype(F32)
    wext[0] = spread + half
    wext[1] = 1.0 - 2.0 * spread
    wext[2] = spread - half
    @pl.when(starts)
    def _():
        for copy in u_halos:
            copy.wait_recv()

    def advance(v, weights, forced):
        west, centre, east = weights
        rows = v.shape[0]
        mixed = centre * v + east * pltpu.roll(v, rows - 1, 0) + west * pltpu.roll(v, 1, 0)
        if forced is not None:
            mixed = mixed + forced
        return dot3(mixed, mh[...], ml[...])

    def weights64():
        return tuple(wext[i, 8:72, :] for i in range(3))

    def sweep(v, weights, forced):
        def turn(k, v):
            return advance(v, weights(), fext[k] if forced else None)
        return lax.fori_loop(0, STEPS, turn, v)

    def weights128():
        return tuple(jnp.concatenate([w, w], axis=0) for w in weights64())

    def weights80():
        return tuple(wext[i] for i in range(3))

    def shift(src, dst, at):
        return [
            remote(src, dst.at[pl.ds(INNER, SLAB)], sh_send.at[at], sh_recv.at[at], p + 1, s),
            remote(src.at[pl.ds(0, INNER)], dst.at[pl.ds(INNER + SLAB, INNER)],
                   sh_send.at[at + 1], sh_recv.at[at + 1], p + 1, up),
            remote(src.at[pl.ds(SLAB - INNER, INNER)], dst.at[pl.ds(0, INNER)],
                   sh_send.at[at + 2], sh_recv.at[at + 2], p + 1, down),
        ]

    def start_shift(copies):
        @pl.when(p < NTM - 1)
        def _():
            for copy in copies:
                copy.start()

    def end_shift(copies, dst):
        @pl.when(p > 0)
        def _():
            for copy in copies:
                copy.wait_recv()

        @pl.when(first)
        def _():
            dst[...] = jnp.zeros_like(dst)

    def arrive(copies):
        @pl.when(p > 0)
        def _():
            for copy in copies:
                copy.wait_recv()

    def turn_before(k, v):
        return advance(v, weights80(), fprev[k].astype(F32))

    arrive(ahead[:3])
    v = jnp.where(p == 1, uin[...], jnp.zeros((80, NY), F32))
    v = lax.fori_loop(0, half_steps, turn_before, v)
    chold[...] = v
    arrive(ahead[3:])
    v = lax.fori_loop(half_steps, STEPS, turn_before, chold[...])
    brecv[...] = v[8:72]
    dsend[...] = sweep(v[8:72], weights64, False)[8:56]
    d_copies = shift(dsend, drecv, 6)

    def forward(which, rows):
        for g in range(GROUPS):
            flat[pl.ds(g, SLAB, stride=GROUPS), :] = rows[:, g * LANES:(g + 1) * LANES]
        fwd_send[which] = flat[...].astype(BF16)
        mine = pl.ds(pl.multiple_of(p * TILE, TILE), TILE)
        for j in range(OWNERS):
            part = pl.ds(j * TILE, TILE)
            copy = remote(fwd_send.at[which, part], fwd_recv.at[which, mine],
                          fs_sem.at[which], fr_sem.at[which], owner_of(j), s)

            @pl.when(p != owner_of(j))
            def _():
                copy.start()

            @pl.when(p == owner_of(j))
            def _():
                fwd_recv[which, mine, :] = fwd_send[which, part, :]

    def forward_end(which):
        def wait(n):
            remote(fwd_send.at[which, pl.ds(0, n * TILE)], fwd_recv.at[which, pl.ds(0, n * TILE)],
                   fs_sem.at[which], fr_sem.at[which], p, up).wait_send()

        @pl.when(is_owner)
        def _():
            wait(OWNERS - 1)

        @pl.when(jnp.logical_not(is_owner))
        def _():
            wait(OWNERS)

    def scan(which, delay, result):
        count = (NTM - 1) * TILE
        remote(fwd_recv.at[which, pl.ds(0, count)], fwd_recv.at[which, pl.ds(0, count)],
               fs_sem.at[which], fr_sem.at[which], p, up).wait_recv()
        flat2[...] = fwd_recv[which].astype(F32)
        size = NTM * ROWS
        total = jnp.concatenate([flat2[pl.ds(g, size, stride=GROUPS), :] for g in range(GROUPS)], axis=1)
        row = lax.broadcasted_iota(jnp.int32, (size, NY), 0)

        def later(x, blocks):
            return jnp.where(row >= blocks * ROWS, pltpu.roll(x, blocks * ROWS, 0), 0.0)

        total = later(total, delay)
        for k in range(5):
            total = total + dot(later(total, 1 << k).astype(BF16), pw[k])
        for g in range(GROUPS):
            flat2[pl.ds(g, size, stride=GROUPS), :] = total[:, g * LANES:(g + 1) * LANES]
        result[...] = flat2[...].astype(result.dtype)

    def back(which, src, dst, edge, top, bottom):
        def copy(block, place, space):
            return remote(src.at[pl.ds(pl.multiple_of(block * TILE, TILE), TILE)],
                          dst.at[pl.ds(pl.multiple_of(place * TILE, TILE), TILE)],
                          bks_sem.at[which], bkr_sem.at[which], block, space)

        @pl.when(top)
        def _():
            @pl.loop(0, NTM)
            def _(i):
                copy(i, edge + OWNERS + chunk, up).start()

        @pl.when(bottom)
        def _():
            @pl.loop(0, NTM)
            def _(i):
                copy(i, chunk - (OWNERS - edge), down).start()

        @pl.loop(1, NTM)
        def _(i):
            copy(lax.rem(p + i, NTM), edge + chunk, s).start()

        at = pl.ds(pl.multiple_of((edge + chunk) * TILE, TILE), TILE)
        dst[at, :] = src[pl.ds(pl.multiple_of(p * TILE, TILE), TILE), :]

    def back_wait(which, dst, edge):
        def wait(n):
            part = dst.at[pl.ds(0, n * TILE)]
            remote(part, part, bks_sem.at[which], bkr_sem.at[which], p, up).wait_recv()

        @pl.when(is_owner)
        def _():
            wait(OWNERS + 2 * edge - 1)

        @pl.when(jnp.logical_not(is_owner))
        def _():
            wait(OWNERS + 2 * edge)

    def back_end(which, src, on_edge):
        def wait(n):
            part = src.at[pl.ds(0, n * TILE)]
            remote(part, part, bks_sem.at[which], bkr_sem.at[which], p, up).wait_send()

        @pl.when(is_owner)
        def _():
            wait(NTM - 1)

        @pl.when(on_edge)
        def _():
            wait(NTM)

    forward(0, dsend[...])
    start_shift(d_copies)

    for copy in halos[:2]:
        copy.wait_recv()
    for side, at in ((0, 0), (1, INNER + SLAB)):
        packed = fhalo[side].astype(F32)
        for k in range(STEPS):
            if k < 4:
                rows = packed[8 * k:8 * k + 8]
            elif k < 7:
                rows = packed[8 * (6 - k):8 * (7 - k)]
                rows = pltpu.roll(rows, INNER - (7 - k) if side == 0 else 7 - k, 0)
            else:
                rows = jnp.zeros((INNER, NY), F32)
            fext[k, at:at + INNER, :] = rows

    begin = jnp.where(first, uin[8:72, :], jnp.zeros((64, NY), F32))
    bsend[...] = sweep(begin, weights64, True)[8:56]

    @pl.when(is_owner)
    def _():
        scan(0, 2, back1_send)
        back(0, back1_send, back1_recv, 4, top_owner, bottom_owner)

    back_wait(0, back1_recv, 4)
    flat3[...] = back1_recv[...].astype(F32)
    before = jnp.concatenate([flat3[pl.ds(g, 80, stride=GROUPS), :] for g in range(GROUPS)], axis=1)

    carry[...] = dot3(before[8:72], pw[0], cl[...])
    v = advance(before, weights80(), None)
    previous_w = lax.fori_loop(1, STEPS, lambda k, v: advance(v, weights80(), None), v)[8:72]
    end_shift(d_copies, drecv)
    carried = carry[...]
    pair = jnp.concatenate([previous_w - carried, drecv[...] + carried], axis=0)
    drecv[...] = brecv[...] + drecv[...] + previous_w
    pair = sweep(pair, weights128, False)
    residual = pair[8:56]
    forward(1, residual)
    out[7] = bsend[...] + dsend[...] + pair[72:120] + residual

    @pl.when(is_owner)
    def _():
        scan(1, 1, back2_send)
        back(1, back2_send, back2_recv, 2, top2_owner, bottom2_owner)

    back_wait(1, back2_recv, 2)
    correction = jnp.concatenate([back2_recv[pl.ds(g, 64, stride=GROUPS), :] for g in range(GROUPS)], axis=1)
    v = jnp.where(first, uin[8:72, :], drecv[...] + correction)
    end = out[7] + dot3(correction[8:56], pw[0], cl[...])
    v = advance(v, weights64(), fext[0])
    out[7] = end
    out[0] = v[8:56]

    def last(k, v):
        v = advance(v, weights64(), fext[k])
        out[k] = v[8:56]
        return v

    lax.fori_loop(1, STEPS - 1, last, v)

    for sent in halos:
        sent.wait_send()

    @pl.when(starts)
    def _():
        for sent in u_halos:
            sent.wait_send()

    @pl.when(p < NTM - 1)
    def _():
        for sent in ahead + d_copies:
            sent.wait_send()

    forward_end(0)
    forward_end(1)
    back_end(0, back1_send, top_owner | bottom_owner)
    back_end(1, back2_send, top2_owner | bottom2_owner)


def per_device(initial_state, velocity, diffusion, forcing, implicit, coarse_implicit):
    V = pltpu.VMEM
    DMA = pltpu.SemaphoreType.DMA
    square = (NY, NY)
    scratch = [
        V(square, F32), V(square, F32), V(square, BF16), V(square, BF16), V(square, BF16),
        V((5,) + square, BF16), V(square, BF16), V(square, F32),
        V((STEPS, SLAB, NY), BF16), V((80, NY), BF16), V((80, NY), BF16), V((80, NY), F32),
        V((2, 32, NY), BF16), V((2, 32, NY), BF16),
        V((3, 80, NY), F32), V((STEPS, 64, NY), F32),
        V((STEPS, 80, NY), BF16),
        V((SLAB, NY), F32), V((64, NY), F32), V((SLAB, NY), F32), V((64, NY), F32),
        V((SLAB * GROUPS, LANES), F32), V((2, SLAB * GROUPS, LANES), BF16),
        V((2, NTM * TILE, LANES), BF16), V((NTM * TILE, LANES), F32),
        V((NTM * TILE, LANES), BF16), V((80 * GROUPS, LANES), BF16), V((80 * GROUPS, LANES), F32),
        V((NTM * TILE, LANES), F32), V((64 * GROUPS, LANES), F32), V((80, NY), F32), V((64, NY), F32),
        DMA((6,)), DMA((6,)), DMA((6,)), DMA((2,)), DMA((2,)), DMA((9,)), DMA((9,)),
        DMA((2,)), DMA((2,)), DMA((2,)), DMA((2,)),
    ]
    return pl.pallas_call(
        kernel,
        out_shape=jax.ShapeDtypeStruct((STEPS, SLAB, NY), F32),
        in_specs=[pl.BlockSpec(memory_space=pl.ANY)] * 6,
        out_specs=pl.BlockSpec(memory_space=pltpu.VMEM),
        scratch_shapes=scratch,
        compiler_params=pltpu.CompilerParams(
            collective_id=0, has_side_effects=True, vmem_limit_bytes=40 * 2**20),
    )(*[pltpu.with_memory_space_constraint(x, pltpu.HBM)
        for x in (initial_state, velocity, diffusion, forcing, implicit, coarse_implicit)])


def solution(mesh):
    in_specs = (
        P("space", None),
        P("space", None),
        P("space", None),
        P("tm", "space", None),
        P(),
        P(),
    )
    return jax.shard_map(
        per_device, mesh=mesh, in_specs=in_specs, out_specs=P("tm", "space", None), check_vma=False
    )
```

time: 75.6 us -> 80.2 us (1.061); the launches traced: 74.4 us -> 80.1 us
  Pallas kernels: 73.5 us -> 79.2 us
    pallas_call x1, Pallas kernels: 73.5 us -> 79.2 us  [per_device(): pl.pallas_call(kernel, out_shape=jax.ShapeDtypeStruct((STEPS, SLAB, NY),...]
where the time goes in v3:
time: 80.2 us; the launch traced here: 80.1 us
  Pallas kernels  79.2 us (99%)
  local copies, waits for them, and re-layouts  0.88 us (1%)
    pallas_call x1, Pallas kernels, per_device(): pl.pallas_call(kernel, out_shape=jax.ShapeDtypeStruct((STEPS, SLAB, NY),...  79.2 us

profile of v3, /device:TPU:1, one launch (start us, length us, event | category | flops | bytes accessed | tf_op | source)
XLA Modules:
  0.0 80.1 jit_solution(17046046325391068698)
XLA Ops:
  0.0 79.2 %shard_map.64 = f32[8,48,512]{2,1,0:T(8,128)S(1)} custom-call(f32[48,512]{1,0:T(8,128)} %u0_hbm.1, bf16[48,512]{1,0:T(8,128)(2,1)} %vel_hbm.1, bf16[48,512]{1,0:T(8,128)(2,1)} %dif_hbm.1, bf16[8,48,512]{2,1,0:T(8,128)(2,1)} %forcing_hbm.1, f32[512,512]{1,0:T(8,128)} %imp_hbm.1, f32[512,512]{1,0:T(8,128)} %coarse_hbm.1), custom_call_target="tpu_custom_call" | custom-call | tf_op jit(solution)/shard_map/pallas_call | solution.py:513
  79.2 0.9 %copy.8 = f32[8,48,512]{2,1,0:T(8,128)} copy(f32[8,48,512]{2,1,0:T(8,128)S(1)} %shard_map.64) | data formatting | bytes 1572864

commit v4 on v2

--- a/solution.py
+++ b/solution.py
@@ -86,24 +86,10 @@
     greet(p, up)
     greet(p, down)
 
-    @pl.when(p < NTM - 1)
-    def _():
-        for other in (up, s, down):
-            greet(p + 1, other)
-
     @pl.when(p > 0)
     def _():
         for other in (up, s, down):
             greet(p - 1, other)
-
-    for j in range(OWNERS):
-        @pl.when(p != owner_of(j))
-        def _():
-            greet(owner_of(j), s)
-        if j < 4:
-            greet(owner_of(j), down)
-        if j >= OWNERS - 4:
-            greet(owner_of(j), up)
 
     @pl.when(is_owner)
     def _():
@@ -111,21 +97,7 @@
         def _(i):
             greet(lax.rem(p + i, NTM), s)
 
-    @pl.when(top_owner)
-    def _():
-        @pl.loop(0, NTM)
-        def _(i):
-            greet(i, up)
-
-    @pl.when(bottom_owner)
-    def _():
-        @pl.loop(0, NTM)
-        def _(i):
-            greet(i, down)
-
-    total = (2 + 12 + 8 + jnp.where(p < NTM - 1, 3, 0) + jnp.where(p > 0, 3, 0)
-             + jnp.where(is_owner, NTM - 2, 0)
-             + jnp.where(top_owner, NTM, 0) + jnp.where(bottom_owner, NTM, 0))
+    total = 2 + OWNERS - jnp.where(is_owner, 1, 0) + jnp.where(p < NTM - 1, 3, 0)
     pl.semaphore_wait(barrier, total)
 
     def remote(src, dst, send, recv, tm, space):
@@ -405,11 +377,12 @@
     back_wait(0, back1_recv, 4)
     flat3[...] = back1_recv[...].astype(F32)
     before = jnp.concatenate([flat3[pl.ds(g, 80, stride=GROUPS), :] for g in range(GROUPS)], axis=1)
-    chold[...] = before
-
-    previous_w = sweep(before, weights80, False)[8:72]
+
+    chold[...] = dot3(before[8:72], pw[0], cl[...])
+    v = advance(before, weights80(), None)
+    previous_w = lax.fori_loop(1, STEPS, lambda k, v: advance(v, weights80(), None), v)[8:72]
     end_shift(d_copies, drecv)
-    carried = dot3(chold[8:72, :], pw[0], cl[...])
+    carried = chold[...]
     pair = jnp.concatenate([previous_w - carried, drecv[...] + carried], axis=0)
     drecv[...] = brecv[...] + drecv[...] + previous_w
     pair = sweep(pair, weights128, False)
@@ -425,14 +398,17 @@
     back_wait(1, back2_recv, 2)
     correction = jnp.concatenate([back2_recv[pl.ds(g, 64, stride=GROUPS), :] for g in range(GROUPS)], axis=1)
     v = jnp.where(first, uin[...], drecv[...] + correction)
-    out[7] = out[7] + dot3(correction[8:56], pw[0], cl[...])
+    end = out[7] + dot3(correction[8:56], pw[0], cl[...])
+    v = advance(v, weights64(), fext[0])
+    out[7] = end
+    out[0] = v[8:56]
 
     def last(k, v):
         v = advance(v, weights64(), fext[k])
         out[k] = v[8:56]
         return v
 
-    lax.fori_loop(0, STEPS - 1, last, v)
+    lax.fori_loop(1, STEPS - 1, last, v)
 
     for sent in halos:
         sent.wait_send()
@@ -467,7 +443,7 @@
         V((SLAB * GROUPS, LANES), F32), V((2, SLAB * GROUPS, LANES), BF16),
         V((2, NTM * TILE, LANES), BF16), V((NTM * TILE, LANES), F32),
         V((NTM * TILE, LANES), BF16), V((80 * GROUPS, LANES), BF16), V((80 * GROUPS, LANES), F32),
-        V((NTM * TILE, LANES), F32), V((64 * GROUPS, LANES), F32), V((80, NY), F32),
+        V((NTM * TILE, LANES), F32), V((64 * GROUPS, LANES), F32), V((64, NY), F32),
         DMA((6,)), DMA((6,)), DMA((6,)), DMA((2,)), DMA((2,)), DMA((6,)), DMA((6,)),
         DMA((2,)), DMA((2,)), DMA((2,)), DMA((2,)),
     ]

time: 75.6 us -> 72.7 us (0.962); the launches traced: 74.4 us -> 72.5 us
  Pallas kernels: 73.5 us -> 71.7 us
    pallas_call x1, Pallas kernels: 73.5 us -> 71.7 us  [per_device(): pl.pallas_call(kernel, out_shape=jax.ShapeDtypeStruct((STEPS, SLAB, NY),...]
where the time goes in v4:
time: 72.7 us; the launch traced here: 72.5 us
  Pallas kernels  71.7 us (99%)
  local copies, waits for them, and re-layouts  0.88 us (1%)
    pallas_call x1, Pallas kernels, per_device(): pl.pallas_call(kernel, out_shape=jax.ShapeDtypeStruct((STEPS, SLAB, NY),...  71.7 us

profile of v4, /device:TPU:1, one launch (start us, length us, event | category | flops | bytes accessed | tf_op | source)
XLA Modules:
  0.0 72.5 jit_solution(15465504885851377392)
XLA Ops:
  0.0 71.7 %shard_map.64 = f32[8,48,512]{2,1,0:T(8,128)S(1)} custom-call(f32[48,512]{1,0:T(8,128)} %u0_hbm.1, bf16[48,512]{1,0:T(8,128)(2,1)} %vel_hbm.1, bf16[48,512]{1,0:T(8,128)(2,1)} %dif_hbm.1, bf16[8,48,512]{2,1,0:T(8,128)(2,1)} %forcing_hbm.1, f32[512,512]{1,0:T(8,128)} %imp_hbm.1, f32[512,512]{1,0:T(8,128)} %coarse_hbm.1), custom_call_target="tpu_custom_call" | custom-call | tf_op jit(solution)/shard_map/pallas_call | solution.py:450
  71.7 0.9 %copy.8 = f32[8,48,512]{2,1,0:T(8,128)} copy(f32[8,48,512]{2,1,0:T(8,128)S(1)} %shard_map.64) | data formatting | bytes 1572864

commit v5 on v4

--- a/solution.py
+++ b/solution.py
@@ -49,7 +49,7 @@
 def kernel(u0_hbm, vel_hbm, dif_hbm, forcing_hbm, imp_hbm, coarse_hbm, out,
            mv, cv, mh, ml, cl, pw, plow, ptmp, fin, vin, din, uin, fpack, fhalo,
            wext, fext, bsend, brecv, dsend, drecv, flat, fwd_send, fwd_recv, flat2,
-           back1_send, back1_recv, flat3, back2_send, back2_recv, chold,
+           back1_send, back1_recv, flat3, back2_send, back2_recv, chold, whold,
            in_sem, halo_send, halo_recv, u_send, u_recv, sh_send, sh_recv,
            fs_sem, fr_sem, bks_sem, bkr_sem):
     p = lax.axis_index("tm")
@@ -220,9 +220,6 @@
             return advance(v, weights(), fext[k] if forced else None)
         return lax.fori_loop(0, STEPS, turn, v)
 
-    def weights128():
-        return tuple(jnp.concatenate([w, w], axis=0) for w in weights64())
-
     def weights80():
         return tuple(wext[i] for i in range(3))
 
@@ -381,14 +378,13 @@
     chold[...] = dot3(before[8:72], pw[0], cl[...])
     v = advance(before, weights80(), None)
     previous_w = lax.fori_loop(1, STEPS, lambda k, v: advance(v, weights80(), None), v)[8:72]
+    whold[...] = previous_w
+    residual = sweep(previous_w - chold[...], weights64, False)[8:56]
+    forward(1, residual)
+    out[7] = bsend[...] + dsend[...] + residual
     end_shift(d_copies, drecv)
-    carried = chold[...]
-    pair = jnp.concatenate([previous_w - carried, drecv[...] + carried], axis=0)
-    drecv[...] = brecv[...] + drecv[...] + previous_w
-    pair = sweep(pair, weights128, False)
-    residual = pair[8:56]
-    forward(1, residual)
-    out[7] = bsend[...] + dsend[...] + pair[72:120] + residual
+    out[7] = out[7] + sweep(drecv[...] + chold[...], weights64, False)[8:56]
+    drecv[...] = brecv[...] + drecv[...] + whold[...]
 
     @pl.when(is_owner)
     def _():
@@ -443,7 +439,7 @@
         V((SLAB * GROUPS, LANES), F32), V((2, SLAB * GROUPS, LANES), BF16),
         V((2, NTM * TILE, LANES), BF16), V((NTM * TILE, LANES), F32),
         V((NTM * TILE, LANES), BF16), V((80 * GROUPS, LANES), BF16), V((80 * GROUPS, LANES), F32),
-        V((NTM * TILE, LANES), F32), V((64 * GROUPS, LANES), F32), V((64, NY), F32),
+        V((NTM * TILE, LANES), F32), V((64 * GROUPS, LANES), F32), V((64, NY), F32), V((64, NY), F32),
         DMA((6,)), DMA((6,)), DMA((6,)), DMA((2,)), DMA((2,)), DMA((6,)), DMA((6,)),
         DMA((2,)), DMA((2,)), DMA((2,)), DMA((2,)),
     ]

time: 72.7 us -> 71.9 us (0.989)
  Pallas kernels: 71.7 us -> 70.9 us
    pallas_call x1, Pallas kernels: 71.7 us -> 70.9 us  [per_device(): pl.pallas_call(kernel, out_shape=jax.ShapeDtypeStruct((STEPS, SLAB, NY),...]
where the time goes in v5:
time: 71.9 us; the launch traced here: 71.8 us
  Pallas kernels  70.9 us (99%)
  local copies, waits for them, and re-layouts  0.88 us (1%)
    pallas_call x1, Pallas kernels, per_device(): pl.pallas_call(kernel, out_shape=jax.ShapeDtypeStruct((STEPS, SLAB, NY),...  70.9 us

profile of v5, /device:TPU:1, one launch (start us, length us, event | category | flops | bytes accessed | tf_op | source)
XLA Modules:
  0.0 71.8 jit_solution(11675400267500954923)
XLA Ops:
  0.0 70.9 %shard_map.64 = f32[8,48,512]{2,1,0:T(8,128)S(1)} custom-call(f32[48,512]{1,0:T(8,128)} %u0_hbm.1, bf16[48,512]{1,0:T(8,128)(2,1)} %vel_hbm.1, bf16[48,512]{1,0:T(8,128)(2,1)} %dif_hbm.1, bf16[8,48,512]{2,1,0:T(8,128)(2,1)} %forcing_hbm.1, f32[512,512]{1,0:T(8,128)} %imp_hbm.1, f32[512,512]{1,0:T(8,128)} %coarse_hbm.1), custom_call_target="tpu_custom_call" | custom-call | tf_op jit(solution)/shard_map/pallas_call | solution.py:446
  70.9 0.9 %copy.8 = f32[8,48,512]{2,1,0:T(8,128)} copy(f32[8,48,512]{2,1,0:T(8,128)S(1)} %shard_map.64) | data formatting | bytes 1572864

commit v6 on v5

--- a/solution.py
+++ b/solution.py
@@ -49,7 +49,7 @@
 def kernel(u0_hbm, vel_hbm, dif_hbm, forcing_hbm, imp_hbm, coarse_hbm, out,
            mv, cv, mh, ml, cl, pw, plow, ptmp, fin, vin, din, uin, fpack, fhalo,
            wext, fext, bsend, brecv, dsend, drecv, flat, fwd_send, fwd_recv, flat2,
-           back1_send, back1_recv, flat3, back2_send, back2_recv, chold, whold,
+           back1_send, back1_recv, flat3, back2_send, back2_recv, edge_send, edge_recv, chold, whold,
            in_sem, halo_send, halo_recv, u_send, u_recv, sh_send, sh_recv,
            fs_sem, fr_sem, bks_sem, bkr_sem):
     p = lax.axis_index("tm")
@@ -318,17 +318,18 @@
                           dst.at[pl.ds(pl.multiple_of(place * TILE, TILE), TILE)],
                           bks_sem.at[which], bkr_sem.at[which], block, space)
 
-        @pl.when(top)
-        def _():
-            @pl.loop(0, NTM)
-            def _(i):
-                copy(i, edge + OWNERS + chunk, up).start()
-
-        @pl.when(bottom)
-        def _():
-            @pl.loop(0, NTM)
-            def _(i):
-                copy(i, chunk - (OWNERS - edge), down).start()
+        if edge:
+            @pl.when(top)
+            def _():
+                @pl.loop(0, NTM)
+                def _(i):
+                    copy(i, edge + OWNERS + chunk, up).start()
+
+            @pl.when(bottom)
+            def _():
+                @pl.loop(0, NTM)
+                def _(i):
+                    copy(i, chunk - (OWNERS - edge), down).start()
 
         @pl.loop(1, NTM)
         def _(i):
@@ -350,18 +351,36 @@
         def _():
             wait(OWNERS + 2 * edge)
 
-    def back_end(which, src, on_edge):
-        def wait(n):
+    def back_end(which, edge_which, src, on_edge):
+        def wait(n, src, which):
             part = src.at[pl.ds(0, n * TILE)]
             remote(part, part, bks_sem.at[which], bkr_sem.at[which], p, up).wait_send()
 
         @pl.when(is_owner)
         def _():
-            wait(NTM - 1)
+            wait(NTM - 1, src, which)
 
         @pl.when(on_edge)
         def _():
-            wait(NTM)
+            wait(NTM, edge_send if edge_which == 2 else src, edge_which)
+
+    def back_edges(src, dst, top, bottom):
+        def copy(block, place, space):
+            return remote(src.at[pl.ds(pl.multiple_of(block * TILE, TILE), TILE)],
+                          dst.at[pl.ds(pl.multiple_of(place * TILE, TILE), TILE)],
+                          bks_sem.at[2], bkr_sem.at[2], block, space)
+
+        @pl.when(top)
+        def _():
+            @pl.loop(0, NTM)
+            def _(i):
+                copy(i, 2 + chunk, up).start()
+
+        @pl.when(bottom)
+        def _():
+            @pl.loop(0, NTM)
+            def _(i):
+                copy(i, chunk - (OWNERS - 2), down).start()
 
     forward(0, dsend[...])
     start_shift(d_copies)
@@ -389,12 +408,18 @@
     @pl.when(is_owner)
     def _():
         scan(1, 1, back2_send)
-        back(1, back2_send, back2_recv, 2, top2_owner, bottom2_owner)
-
-    back_wait(1, back2_recv, 2)
-    correction = jnp.concatenate([back2_recv[pl.ds(g, 64, stride=GROUPS), :] for g in range(GROUPS)], axis=1)
+        edge_send[...] = back2_send[...].astype(BF16)
+        back_edges(edge_send, edge_recv, top2_owner, bottom2_owner)
+        back(1, back2_send, back2_recv, 0, None, None)
+
+    back_wait(1, back2_recv, 0)
+    own = jnp.concatenate([back2_recv[pl.ds(g, SLAB, stride=GROUPS), :] for g in range(GROUPS)], axis=1)
+    remote(edge_recv, edge_recv, bks_sem.at[2], bkr_sem.at[2], p, up).wait_recv()
+    flat3[0:4 * TILE, :] = edge_recv[...].astype(F32)
+    beside = jnp.concatenate([flat3[pl.ds(g, 16, stride=GROUPS), :] for g in range(GROUPS)], axis=1)
+    correction = jnp.concatenate([beside[:8], own, beside[8:]], axis=0)
     v = jnp.where(first, uin[...], drecv[...] + correction)
-    end = out[7] + dot3(correction[8:56], pw[0], cl[...])
+    end = out[7] + dot3(own, pw[0], cl[...])
     v = advance(v, weights64(), fext[0])
     out[7] = end
     out[0] = v[8:56]
@@ -421,8 +446,8 @@
 
     forward_end(0)
     forward_end(1)
-    back_end(0, back1_send, top_owner | bottom_owner)
-    back_end(1, back2_send, top2_owner | bottom2_owner)
+    back_end(0, 0, back1_send, top_owner | bottom_owner)
+    back_end(1, 2, back2_send, top2_owner | bottom2_owner)
 
 
 def per_device(initial_state, velocity, diffusion, forcing, implicit, coarse_implicit):
@@ -439,9 +464,10 @@
         V((SLAB * GROUPS, LANES), F32), V((2, SLAB * GROUPS, LANES), BF16),
         V((2, NTM * TILE, LANES), BF16), V((NTM * TILE, LANES), F32),
         V((NTM * TILE, LANES), BF16), V((80 * GROUPS, LANES), BF16), V((80 * GROUPS, LANES), F32),
-        V((NTM * TILE, LANES), F32), V((64 * GROUPS, LANES), F32), V((64, NY), F32), V((64, NY), F32),
+        V((NTM * TILE, LANES), F32), V((SLAB * GROUPS, LANES), F32),
+        V((NTM * TILE, LANES), BF16), V((4 * TILE, LANES), BF16), V((64, NY), F32), V((64, NY), F32),
         DMA((6,)), DMA((6,)), DMA((6,)), DMA((2,)), DMA((2,)), DMA((6,)), DMA((6,)),
-        DMA((2,)), DMA((2,)), DMA((2,)), DMA((2,)),
+        DMA((2,)), DMA((2,)), DMA((3,)), DMA((3,)),
     ]
     return pl.pallas_call(
         kernel,

time: 71.9 us -> 70.2 us (0.976)
  Pallas kernels: 70.9 us -> 69.2 us
    pallas_call x1, Pallas kernels: 70.9 us -> 69.2 us  [per_device(): pl.pallas_call(kernel, out_shape=jax.ShapeDtypeStruct((STEPS, SLAB, NY),...]
where the time goes in v6:
time: 70.2 us; the launch traced here: 70 us
  Pallas kernels  69.2 us (99%)
  local copies, waits for them, and re-layouts  0.88 us (1%)
    pallas_call x1, Pallas kernels, per_device(): pl.pallas_call(kernel, out_shape=jax.ShapeDtypeStruct((STEPS, SLAB, NY),...  69.2 us

profile of v6, /device:TPU:1, one launch (start us, length us, event | category | flops | bytes accessed | tf_op | source)
XLA Modules:
  0.0 70.0 jit_solution(5346510573749152225)
XLA Ops:
  0.0 69.2 %shard_map.64 = f32[8,48,512]{2,1,0:T(8,128)S(1)} custom-call(f32[48,512]{1,0:T(8,128)} %u0_hbm.1, bf16[48,512]{1,0:T(8,128)(2,1)} %vel_hbm.1, bf16[48,512]{1,0:T(8,128)(2,1)} %dif_hbm.1, bf16[8,48,512]{2,1,0:T(8,128)(2,1)} %forcing_hbm.1, f32[512,512]{1,0:T(8,128)} %imp_hbm.1, f32[512,512]{1,0:T(8,128)} %coarse_hbm.1), custom_call_target="tpu_custom_call" | custom-call | tf_op jit(solution)/shard_map/pallas_call | solution.py:472
  69.2 0.9 %copy.8 = f32[8,48,512]{2,1,0:T(8,128)} copy(f32[8,48,512]{2,1,0:T(8,128)S(1)} %shard_map.64) | data formatting | bytes 1572864

commit v7 on v6

--- a/solution.py
+++ b/solution.py
@@ -49,7 +49,7 @@
 def kernel(u0_hbm, vel_hbm, dif_hbm, forcing_hbm, imp_hbm, coarse_hbm, out,
            mv, cv, mh, ml, cl, pw, plow, ptmp, fin, vin, din, uin, fpack, fhalo,
            wext, fext, bsend, brecv, dsend, drecv, flat, fwd_send, fwd_recv, flat2,
-           back1_send, back1_recv, flat3, back2_send, back2_recv, edge_send, edge_recv, chold, whold,
+           back1_send, back1_recv, flat3, back2_send, back2_recv, edge_send, edge_recv, edge_out, edge_in, chold, whold,
            in_sem, halo_send, halo_recv, u_send, u_recv, sh_send, sh_recv,
            fs_sem, fr_sem, bks_sem, bkr_sem):
     p = lax.axis_index("tm")
@@ -224,12 +224,14 @@
         return tuple(wext[i] for i in range(3))
 
     def shift(src, dst, at):
+        which = at // 3
+        for side, start in ((0, 0), (1, SLAB - INNER)):
+            rows = src[start:start + INNER, :]
+            edge_out[which, side] = jnp.concatenate([rows[:, :NY // 2], rows[:, NY // 2:]], axis=0).astype(BF16)
         return [
             remote(src, dst.at[pl.ds(INNER, SLAB)], sh_send.at[at], sh_recv.at[at], p + 1, s),
-            remote(src.at[pl.ds(0, INNER)], dst.at[pl.ds(INNER + SLAB, INNER)],
-                   sh_send.at[at + 1], sh_recv.at[at + 1], p + 1, up),
-            remote(src.at[pl.ds(SLAB - INNER, INNER)], dst.at[pl.ds(0, INNER)],
-                   sh_send.at[at + 2], sh_recv.at[at + 2], p + 1, down),
+            remote(edge_out.at[which, 0], edge_in.at[which, 1], sh_send.at[at + 1], sh_recv.at[at + 1], p + 1, up),
+            remote(edge_out.at[which, 1], edge_in.at[which, 0], sh_send.at[at + 2], sh_recv.at[at + 2], p + 1, down),
         ]
 
     def start_shift(copies):
@@ -238,11 +240,14 @@
             for copy in copies:
                 copy.start()
 
-    def end_shift(copies, dst):
+    def end_shift(copies, dst, which):
         @pl.when(p > 0)
         def _():
             for copy in copies:
                 copy.wait_recv()
+            for side, start in ((0, 0), (1, INNER + SLAB)):
+                rows = edge_in[which, side].astype(F32)
+                dst[start:start + INNER, :] = jnp.concatenate([rows[:INNER], rows[INNER:]], axis=1)
 
         @pl.when(first)
         def _():
@@ -258,7 +263,7 @@
         square(3)
         square(4)
 
-    end_shift(b_copies, brecv)
+    end_shift(b_copies, brecv, 0)
     dsend[...] = sweep(brecv[...], weights64, False)[8:56]
     d_copies = shift(dsend, drecv, 3)
 
@@ -401,7 +406,7 @@
     residual = sweep(previous_w - chold[...], weights64, False)[8:56]
     forward(1, residual)
     out[7] = bsend[...] + dsend[...] + residual
-    end_shift(d_copies, drecv)
+    end_shift(d_copies, drecv, 1)
     out[7] = out[7] + sweep(drecv[...] + chold[...], weights64, False)[8:56]
     drecv[...] = brecv[...] + drecv[...] + whold[...]
 
@@ -465,7 +470,8 @@
         V((2, NTM * TILE, LANES), BF16), V((NTM * TILE, LANES), F32),
         V((NTM * TILE, LANES), BF16), V((80 * GROUPS, LANES), BF16), V((80 * GROUPS, LANES), F32),
         V((NTM * TILE, LANES), F32), V((SLAB * GROUPS, LANES), F32),
-        V((NTM * TILE, LANES), BF16), V((4 * TILE, LANES), BF16), V((64, NY), F32), V((64, NY), F32),
+        V((NTM * TILE, LANES), BF16), V((4 * TILE, LANES), BF16),
+        V((2, 2, 16, NY // 2), BF16), V((2, 2, 16, NY // 2), BF16), V((64, NY), F32), V((64, NY), F32),
         DMA((6,)), DMA((6,)), DMA((6,)), DMA((2,)), DMA((2,)), DMA((6,)), DMA((6,)),
         DMA((2,)), DMA((2,)), DMA((3,)), DMA((3,)),
     ]

time: 70.2 us -> 70.1 us (level)
  no operation moved by 1% of the time
where the time goes in v7:
time: 70.1 us; the launch traced here: 70 us
  Pallas kernels  69.1 us (99%)
  local copies, waits for them, and re-layouts  0.88 us (1%)
    pallas_call x1, Pallas kernels, per_device(): pl.pallas_call(kernel, out_shape=jax.ShapeDtypeStruct((STEPS, SLAB, NY),...  69.1 us

profile of v7, /device:TPU:1, one launch (start us, length us, event | category | flops | bytes accessed | tf_op | source)
XLA Modules:
  0.0 70.0 jit_solution(3929516602780133208)
XLA Ops:
  0.0 69.1 %shard_map.64 = f32[8,48,512]{2,1,0:T(8,128)S(1)} custom-call(f32[48,512]{1,0:T(8,128)} %u0_hbm.1, bf16[48,512]{1,0:T(8,128)(2,1)} %vel_hbm.1, bf16[48,512]{1,0:T(8,128)(2,1)} %dif_hbm.1, bf16[8,48,512]{2,1,0:T(8,128)(2,1)} %forcing_hbm.1, f32[512,512]{1,0:T(8,128)} %imp_hbm.1, f32[512,512]{1,0:T(8,128)} %coarse_hbm.1), custom_call_target="tpu_custom_call" | custom-call | tf_op jit(solution)/shard_map/pallas_call | solution.py:478
  69.1 0.9 %copy.8 = f32[8,48,512]{2,1,0:T(8,128)} copy(f32[8,48,512]{2,1,0:T(8,128)S(1)} %shard_map.64) | data formatting | bytes 1572864
